TPU v7x, 32 devices: a whole 2x2x4 slice. The times are simulated.
32 devices in a mesh: groups: 2 (over y), store: 16 (over z, x, core).
Axes of the slice: x: 2, y: 2, z: 4, core: 2. Of those that a mesh axis runs over, the one named last changes fastest.
Arguments:
- queries: bfloat16 [2, 32, 8192], P(None, ('groups', 'store')), parts along dimension 1, may hold values from -6 to 206
- new_keys: bfloat16 [2, 32, 1024], P(None, ('groups', 'store')), parts along dimension 1, may hold values from -6 to 12.5
- incoming_values: bfloat16 [2, 32, 1024], P(None, ('groups', 'store')), parts along dimension 1, may hold values from -6 to 6
- key_left: bfloat16 [32, 4096, 160], P(('groups', 'store')), parts along dimension 0, may hold values from -12 to 12
- right_key_factor: bfloat16 [32, 160, 1024], P(('groups', 'store')), parts along dimension 0, may hold values from -0.5 to 0.5
- value_tile_store: bfloat16 [131072, 1024], P(('groups', 'store')), parts along dimension 0, may hold values from -6 to 6
- slot_map: int32 [32, 8, 512], P(('groups', 'store')), parts along dimension 0, may hold values from 0 to 65535, as said below
- chosen: int32 [2, 32, 8, 64], P(None, ('groups', 'store')), parts along dimension 1, may hold values from 0 to 511, as said below
- lengths: int32 [32], P(('groups', 'store')), parts along dimension 0, may hold values from 1024 to 4096
Outputs:
- attended: bfloat16 [2, 32, 8192], P(None, ('groups', 'store')), parts along dimension 1
There are 2 independent parts, one for each index of `groups`. A program takes and returns all parts, laid end to end along the dimension named above; each array names one. Nothing has to cross between parts.
Inputs may be any that keep to these rules, and one draw needn't show every extreme that they name: `slot_map`: the entries are distinct; pool rows r * 4096 to (r+1) * 4096 - 1 stand on index r of store. `chosen`: the 64 blocks of one step, request and key head are distinct; at most 8 of them have their slot_map row on one index of store, and in every step some index of store holds exactly 8 of them for every request and key head.
All inputs are finite; a program needn't handle non-finite values.
Results may differ from a plain program's by a relative error of at most 0.005.
The roundings to bfloat16 on the way count: a program that leaves them out, or rounds other values in their place, can miss the bound.
Values may be sent and summed in bfloat16 or wider, within the bound.
No kernel may reach another device: no remote copies, remote signals or barrier semaphores. Data moves between devices by JAX's collectives and lax.ppermute only.
A program may use at most 64 MiB of HBM per device.

v0:
```python
import jax
import jax.numpy as jnp
from jax import lax
from jax.sharding import PartitionSpec as P

KEY_VALUE_HEADS = 8
HEAD_SIZE = 128
BLOCK_TOKENS = 8


ROPE_BASE = 500000.0


def apply_rotary(tensor, token_positions):
    half_dim = tensor.shape[-1] // 2
    inverse = ROPE_BASE ** (-(jnp.arange(half_dim, dtype=jnp.float32) * 2.0 / tensor.shape[-1]))
    angles = jnp.asarray(token_positions).astype(jnp.float32)[..., None] * inverse
    cosine = jnp.cos(angles)
    sine_vals = jnp.sin(angles)
    first_half = tensor[..., :half_dim]
    second_half = tensor[..., half_dim:]
    return jnp.concatenate(
        [
            first_half * cosine - second_half * sine_vals,
            second_half * cosine + first_half * sine_vals,
        ],
        -1,
    )


def fetch_tiles(requests, value_tile_store):
    tile_row_index = jnp.take(
        value_tile_store,
        lax.all_to_all(requests, "store", split_axis=0, concat_axis=0, tiled=True),
        axis=0,
    )
    return lax.all_to_all(tile_row_index, "store", split_axis=0, concat_axis=0, tiled=True)


def build_requests(flat_idx, inside, total):
    buffer = jnp.zeros((total,), jnp.int32)
    return buffer.at[flat_idx.reshape(-1)].set(inside.reshape(-1))


def attend_row(
    query_full,
    incoming_keys_full,
    incoming_values_full,
    left_rows,
    right_factor_rows,
    block_numbers,
    tile_row_index,
    length,
    step_index,
):
    query_group_size = query_full.shape[-1] // HEAD_SIZE // KEY_VALUE_HEADS
    every_head = query_group_size * KEY_VALUE_HEADS
    selected_count = block_numbers.shape[1]
    score_scale = HEAD_SIZE ** (-0.5)
    right_factor_heads = right_factor_rows.reshape(
        right_factor_rows.shape[0], KEY_VALUE_HEADS, HEAD_SIZE
    )
    token_positions = (
        block_numbers[:, :, None] * BLOCK_TOKENS + jnp.arange(BLOCK_TOKENS, dtype=jnp.int32)
    ).reshape(KEY_VALUE_HEADS, selected_count * BLOCK_TOKENS)
    picked = left_rows[token_positions]
    raw_keys = jnp.einsum(
        "htr,rhd->htd", picked, right_factor_heads, preferred_element_type=jnp.float32
    )
    cache_keys = apply_rotary(raw_keys, token_positions).astype(jnp.bfloat16)
    rotated_query = apply_rotary(
        query_full[step_index].reshape(every_head, HEAD_SIZE).astype(jnp.float32),
        length + step_index,
    ).astype(jnp.bfloat16)
    current_position = (length + jnp.arange(step_index + 1, dtype=jnp.int32))[:, None]
    current_keys = apply_rotary(
        incoming_keys_full[: step_index + 1]
        .reshape(step_index + 1, KEY_VALUE_HEADS, HEAD_SIZE)
        .astype(jnp.float32),
        current_position,
    ).astype(jnp.bfloat16)
    current_keys = jnp.transpose(current_keys, (1, 0, 2))
    current_values = jnp.transpose(
        incoming_values_full[: step_index + 1].reshape(step_index + 1, KEY_VALUE_HEADS, HEAD_SIZE),
        (1, 0, 2),
    )
    local_values = tile_row_index.reshape(KEY_VALUE_HEADS, selected_count * BLOCK_TOKENS, HEAD_SIZE)
    grouped_queries = rotated_query.reshape(KEY_VALUE_HEADS, query_group_size, HEAD_SIZE)
    cache_scores = (
        jnp.einsum("hgd,htd->hgt", grouped_queries, cache_keys, preferred_element_type=jnp.float32)
        * score_scale
    )
    inside_len = token_positions < length
    cache_scores = jnp.where(inside_len[:, None, :], cache_scores, -jnp.inf)
    fresh_scores = (
        jnp.einsum(
            "hgd,hnd->hgn", grouped_queries, current_keys, preferred_element_type=jnp.float32
        )
        * score_scale
    )
    highest = jnp.maximum(
        jnp.max(cache_scores, -1, keepdims=True), jnp.max(fresh_scores, -1, keepdims=True)
    )
    cache_exp = jnp.exp(cache_scores - highest)
    fresh_exp = jnp.exp(fresh_scores - highest)
    denominator = jnp.sum(cache_exp, -1, keepdims=True) + jnp.sum(fresh_exp, -1, keepdims=True)
    cache_weight = (cache_exp / denominator).astype(jnp.bfloat16)
    fresh_weight = (fresh_exp / denominator).astype(jnp.bfloat16)
    attended = jnp.einsum(
        "hgt,htd->hgd", cache_weight, local_values, preferred_element_type=jnp.float32
    )
    attended = attended + jnp.einsum(
        "hgn,hnd->hgd", fresh_weight, current_values, preferred_element_type=jnp.float32
    )
    return attended.reshape(every_head * HEAD_SIZE).astype(jnp.bfloat16)


def per_device(
    queries,
    new_keys,
    incoming_values,
    key_left,
    right_key_factor,
    value_tile_store,
    slot_map,
    chosen,
    lengths,
):
    nstore = lax.axis_size("store")
    local_rows = key_left.shape[0]
    nchunk = slot_map.shape[2]
    step_count = chosen.shape[0]
    selected_count = chosen.shape[3]
    keeper_share = max(1, nchunk // nstore // 4)
    tile_limit = local_rows * KEY_VALUE_HEADS * keeper_share
    pool_here = value_tile_store.shape[0]
    slot_numbers = jnp.take_along_axis(
        jnp.broadcast_to(slot_map[None], (step_count,) + slot_map.shape), chosen, axis=3
    )
    tile_keeper = slot_numbers // pool_here
    inside = slot_numbers % pool_here
    matched = tile_keeper[..., :, None] == tile_keeper[..., None, :]
    earlier = jnp.arange(selected_count)[None, :] < jnp.arange(selected_count)[:, None]
    order_in = jnp.sum(jnp.logical_and(matched, earlier), -1)
    row_head = (
        jnp.arange(local_rows, dtype=jnp.int32)[:, None, None] * KEY_VALUE_HEADS
        + jnp.arange(KEY_VALUE_HEADS, dtype=jnp.int32)[None, :, None]
    )
    position = row_head * keeper_share + order_in
    tiles_all = []
    slot_span = step_count * tile_limit
    flat_idx = (
        tile_keeper * slot_span
        + jnp.arange(step_count, dtype=jnp.int32)[:, None, None, None] * tile_limit
        + position
    )
    requests = build_requests(flat_idx, inside, nstore * slot_span).reshape(nstore, slot_span)
    received = fetch_tiles(requests, value_tile_store).reshape(nstore * slot_span, -1)
    for step_index in range(step_count):
        tiles_all.append(received[flat_idx[step_index]])
    results = []
    for step_index in range(step_count):
        per_rows = [
            attend_row(
                queries[:, 0],
                new_keys[:, 0],
                incoming_values[:, 0],
                key_left[0],
                right_key_factor[0],
                chosen[step_index, 0],
                tiles_all[step_index][0],
                lengths[0],
                step_index,
            )
        ]
        results.append(jnp.stack(per_rows))
    return jnp.stack(results)


def solution(mesh):
    in_specs = (
        P(None, ("groups", "store"), None),
        P(None, ("groups", "store"), None),
        P(None, ("groups", "store"), None),
        P(("groups", "store"), None, None),
        P(("groups", "store"), None, None),
        P(("groups", "store"), None),
        P(("groups", "store"), None, None),
        P(None, ("groups", "store"), None, None),
        P(("groups", "store")),
    )
    out_specs = P(None, ("groups", "store"), None)
    return jax.shard_map(
        per_device, mesh=mesh, in_specs=in_specs, out_specs=out_specs, check_vma=False
    )
```

profile of v0, /device:TPU:11, one launch (start us, length us, event | category | flops | bytes accessed | tf_op | source)
XLA Modules:
  0.0 157.6 jit_solution(14860396995195361211)
XLA Ops:
  0.0 0.7 bitcast_or_fusion
  0.8 8.4 %gather_fusion.5 = s32[1024]{0:T(1024)S(1)} fusion(s32[2,8,512]{2,1,0:T(8,128)S(1)} %broadcast.481, s32[1024]{0:T(1024)S(1)} %reshape.724), kind=kCustom, calls=%fused_computation.5 | custom fusion | bytes 20480 | tf_op jit(solution)/shard_map/jit(take_along_axis)/gather | solution.py:137
  9.4 0.5 convert_reduce_fusion
  10.1 4.9 %scatter_custom_fusion = s32[2048]{0:T(1024)} fusion(s32[1024]{0:T(1024)S(1)} %bitcast.150, s32[1024]{0:T(1024)S(1)} %reshape.734, s32[]{:T(128)} %constant.79.clone.1), kind=kCustom, calls=%fused_computation.123 | custom fusion | bytes 8196 | tf_op jit(solution)/shard_map/scatter | solution.py:42
  14.9 6.6 %all-to-all-start = ((s32[16,1,128]{2,1,0:T(1,128)}), s32[16,1,128]{2,1,0:T(1,128)S(1)}, u32[]{:S(2)}, u32[]{:S(2)}) async-start(s32[16,1,128]{2,1,0:T(1,128)} %bitcast.22), calls=%async_computation | async-start | bytes 16384 | tf_op jit(solution)/shard_map/all_to_all | solution.py:34
  21.7 0.2 add.276
  22.0 0.2 add.304
  22.3 3.0 %all-to-all-done = s32[16,1,128]{2,1,0:T(1,128)S(1)} async-done(((s32[16,1,128]{2,1,0:T(1,128)}), s32[16,1,128]{2,1,0:T(1,128)S(1)}, u32[]{:S(2)}, u32[]{:S(2)}) %all-to-all-start) | async-done | bytes 8224 | tf_op jit(solution)/shard_map/all_to_all | solution.py:34
  25.2 15.4 %gather_fusion.1 = bf16[2048,1024]{1,0:T(8,128)(2,1)} fusion(bf16[4096,1024]{1,0:T(8,128)(2,1)} %param.14, s32[2048]{0:T(1024)S(1)} %fusion.44), kind=kCustom, calls=%fused_computation.1 | custom fusion | bytes 8396800 | tf_op jit(solution)/shard_map/jit(_take)/gather | solution.py:32
  40.7 3.8 %broadcast_select_fusion = bf16[16,128,1024]{2,1,0:T(8,128)(2,1)} fusion(bf16[16,128,1024]{2,1,0:T(8,128)(2,1)} %bitcast.131, pred[16,128]{1,0:T(8,128)(4,1)S(1)} %compare_and_fusion), kind=kLoop, calls=%fused_computation.7 | loop fusion | flops 2097152 | bytes 8390656 | tf_op jit(solution)/shard_map/jit(_take)/select_n | solution.py:32
  44.5 7.1 %all-to-all-start.1 = ((bf16[16,128,1024]{2,1,0:T(8,128)(2,1)}), bf16[16,128,1024]{2,1,0:T(8,128)(2,1)}, u32[]{:S(2)}, u32[]{:S(2)}) async-start(bf16[16,128,1024]{2,1,0:T(8,128)(2,1)} %broadcast_select_fusion), calls=%async_computation.1 | async-start | bytes 8388608 | tf_op jit(solution)/shard_map/all_to_all | solution.py:37
  52.8 3.1 %copy.40 = bf16[1,4096,160]{2,1,0:T(8,128)(2,1)S(1)} copy(bf16[1,4096,160]{1,2,0:T(8,128)(2,1)} %param.12) | data formatting | bytes 2621440 | tf_op args[3]
  55.9 16.9 %gather_fusion.3 = bf16[4096,160]{1,0:T(8,128)(2,1)} fusion(bf16[4096,160]{1,0:T(8,128)(2,1)S(1)} %bitcast.129, s32[4096]{0:T(1024)S(1)} %broadcast_clamp_fusion), kind=kCustom, calls=%fused_computation.3 | custom fusion | bytes 2637824 | tf_op jit(solution)/shard_map/gather | solution.py:66
  72.9 16.9 %gather_fusion = bf16[4096,160]{1,0:T(8,128)(2,1)} fusion(bf16[4096,160]{1,0:T(8,128)(2,1)S(1)} %bitcast.130, s32[4096]{0:T(1024)S(1)} %broadcast_clamp_fusion.1), kind=kCustom, calls=%fused_computation | custom fusion | bytes 2637824 | tf_op jit(solution)/shard_map/gather | solution.py:66
  90.2 0.2 fusion.68
  90.5 2.6 %fusion.28 = f32[8,512,128]{1,2,0:T(8,128)S(1)} fusion(bf16[8,512,160]{2,1,0:T(8,128)(2,1)} %bitcast.133, bf16[160,8,128]{2,1,0:T(8,128)(2,1)S(1)} %bitcast.134), kind=kOutput, calls=%fused_computation.46 | convolution fusion | flops 167772160 | bytes 3735552 | tf_op jit(solution)/shard_map/htr,rhd->htd/dot_general | solution.py:67
  93.1 0.8 fusion.26
  93.9 8.2 %fusion.17 = (bf16[8,512,64]{1,2,0:T(8,128)(2,1)S(1)}, bf16[8,512,64]{1,2,0:T(8,128)(2,1)S(1)}, bf16[8,512,64]{1,2,0:T(8,128)(2,1)S(1)}, bf16[8,512,64]{1,2,0:T(8,128)(2,1)S(1)}) fusion(f32[8,512,128]{1,2,0:T(8,128)S(1)} %fusion.28, f32[64]{0:T(128)S(1)} %negate_power_fusion, f32[8,512]{1,0:T(8,128)S(1)} %get-tuple-element.27, ...), kind=kLoop, calls=%fused_computation.34 | loop fusion | flops 4718592 | bytes 6324480 | tf_op jit(solution)/shard_map/convert.20
  102.1 0.4 fusion.67
  102.5 0.2 fusion.31
  103.1 0.2 fusion.56
  103.3 0.4 fusion.69
  103.7 0.2 fusion.30
  103.9 40.2 %all-to-all-done.1 = bf16[16,128,1024]{2,1,0:T(8,128)(2,1)} async-done(((bf16[16,128,1024]{2,1,0:T(8,128)(2,1)}), bf16[16,128,1024]{2,1,0:T(8,128)(2,1)}, u32[]{:S(2)}, u32[]{:S(2)}) %all-to-all-start.1) | async-done | bytes 4194336 | tf_op jit(solution)/shard_map/all_to_all | solution.py:37
  144.1 5.5 %gather_fusion.4 = bf16[512,1024]{1,0:T(8,128)(2,1)S(1)} fusion(bf16[2048,1024]{1,0:T(8,128)(2,1)} %bitcast.27, s32[1024]{0:T(1024)S(1)} %pad_clamp_fusion), kind=kCustom, calls=%fused_computation.4 | custom fusion | bytes 2099200 | tf_op jit(solution)/shard_map/gather | solution.py:160
  149.6 5.5 %gather_fusion.2 = bf16[512,1024]{1,0:T(8,128)(2,1)S(1)} fusion(bf16[2048,1024]{1,0:T(8,128)(2,1)} %bitcast.27, s32[1024]{0:T(1024)S(1)} %pad_clamp_fusion.1), kind=kCustom, calls=%fused_computation.2 | custom fusion | bytes 2099200 | tf_op jit(solution)/shard_map/gather | solution.py:160
  155.0 0.5 reshape_squeeze.17
  155.5 0.5 reshape_squeeze.18
  156.1 0.3 fusion.32
  156.3 0.2 fusion.11
  156.6 0.3 fusion.10
  156.9 0.7 pad_maximum_fusion
  (70 shorter events, 2.2 us)
Async XLA Ops:
  0.0 0.8 copy-start
  0.8 8.5 %copy-start.4 = (s32[2,1,8,64]{3,2,1,0:T(8,128)S(1)}, s32[2,1,8,64]{3,2,1,0:T(8,128)}, u32[]{:S(2)}) copy-start(s32[2,1,8,64]{3,2,1,0:T(8,128)} %param.16) | copy-start | bytes 12292
  14.9 10.3 %all-to-all-start = ((s32[16,1,128]{2,1,0:T(1,128)}), s32[16,1,128]{2,1,0:T(1,128)S(1)}, u32[]{:S(2)}, u32[]{:S(2)}) async-start(s32[16,1,128]{2,1,0:T(1,128)} %bitcast.22), calls=%async_computation | async-start | bytes 16384 | tf_op jit(solution)/shard_map/all_to_all | solution.py:34
  44.5 8.3 %copy-start.2 = (bf16[1,160,1024]{2,1,0:T(8,128)(2,1)S(1)}, bf16[1,160,1024]{2,1,0:T(8,128)(2,1)}, u32[]{:S(2)}) copy-start(bf16[1,160,1024]{2,1,0:T(8,128)(2,1)} %param.13) | copy-start | bytes 983044
  44.5 99.6 %all-to-all-start.1 = ((bf16[16,128,1024]{2,1,0:T(8,128)(2,1)}), bf16[16,128,1024]{2,1,0:T(8,128)(2,1)}, u32[]{:S(2)}, u32[]{:S(2)}) async-start(bf16[16,128,1024]{2,1,0:T(8,128)(2,1)} %broadcast_select_fusion), calls=%async_computation.1 | async-start | bytes 8388608 | tf_op jit(solution)/shard_map/all_to_all | solution.py:37
  72.9 17.1 %copy-start.5 = (bf16[2,1,1024]{2,0,1:T(2,128)(2,1)S(1)}, bf16[2,1,1024]{2,0,1:T(2,128)(2,1)}, u32[]{:S(2)}) copy-start(bf16[2,1,1024]{2,0,1:T(2,128)(2,1)} %param.10) | copy-start | bytes 12292
  72.9 17.2 %copy-start.3 = (bf16[2,1,8192]{2,0,1:T(2,128)(2,1)S(1)}, bf16[2,1,8192]{2,0,1:T(2,128)(2,1)}, u32[]{:S(2)}) copy-start(bf16[2,1,8192]{2,0,1:T(2,128)(2,1)} %param.9) | copy-start | bytes 98308
  90.5 2.6 %copy-start.1 = (bf16[4096,160]{1,0:T(8,128)(2,1)S(1)}, bf16[4096,160]{1,0:T(8,128)(2,1)}, u32[]{:S(2)}) copy-start(bf16[4096,160]{1,0:T(8,128)(2,1)} %gather_fusion.3) | copy-start | bytes 3932164
  102.1 1.8 %copy-start.6 = (bf16[2,1,1024]{2,0,1:T(2,128)(2,1)S(1)}, bf16[2,1,1024]{2,0,1:T(2,128)(2,1)}, u32[]{:S(2)}) copy-start(bf16[2,1,1024]{2,0,1:T(2,128)(2,1)} %param.11) | copy-start | bytes 12292
where the time goes:
time: 158 us
  local copies, waits for them, and re-layouts  79.1 us (50%)
  waiting for transfers between devices  43.2 us (27%)
  other arithmetic  15.2 us (10%)
  starting transfers between devices  13.7 us (9%)
  matrix products  5.36 us (3%)
    all_to_all x1, waiting for transfers between devices, fetch_tiles(): lax.all_to_all(tile_row_index, 'store', split_axis=0, concat_axis=0, tile...  40.2 us
    gather x2, local copies, waits for them, and re-layouts, attend_row(): picked = left_rows[token_positions]  33.8 us
    gather x1, local copies, waits for them, and re-layouts, fetch_tiles(): jnp.take(value_tile_store, lax.all_to_all(requests, 'store', split_axis=0...  15.4 us
    gather x2, local copies, waits for them, and re-layouts, per_device(): tiles_all.append(received[flat_idx[step_index]])  10.9 us
    gather x3, local copies, waits for them, and re-layouts, per_device(): jnp.take_along_axis(jnp.broadcast_to(slot_map[None], (step_count,) + slot...  8.53 us
    another operation x4, other arithmetic  8.28 us
    all_to_all x1, starting transfers between devices, fetch_tiles(): lax.all_to_all(tile_row_index, 'store', split_axis=0, concat_axis=0, tile...  7.14 us
    all_to_all x1, starting transfers between devices, fetch_tiles(): lax.all_to_all(requests, 'store', split_axis=0, concat_axis=0, tiled=True)  6.55 us
  transfers between devices with their start and end apart: 2, of which 2 were waited for; matrix products, arithmetic and copies ran while one was open for 33% of the time, Pallas kernels for 0%

commit v1 on v0

v1 whole, which is shorter than its diff:
```python
import functools

import jax
import jax.numpy as jnp
import numpy as np
from jax import lax
from jax.experimental import pallas as pl
from jax.experimental.pallas import tpu as pltpu
from jax.sharding import PartitionSpec as P

HEAD_SIZE = 128
HALF = HEAD_SIZE // 2
BLOCK_TOKENS = 8
ROPE_BASE = 500000.0
NT = (((1,), (1,)), ((), ()))
NN = (((1,), (0,)), ((), ()))
F32 = jnp.float32
BF16 = jnp.bfloat16


def mm(a, b, dims=NN):
    return lax.dot_general(a, b, dims, preferred_element_type=F32)


def rope_tables(blocks):
    exponent = -(np.arange(HALF, dtype=np.float32) * np.float32(2.0) / np.float32(HEAD_SIZE))
    freq = (np.float32(ROPE_BASE) ** exponent).astype(np.float64)
    freq = np.concatenate([freq, freq])
    rows = np.arange(-(-(blocks + 2) // 8) * 8, dtype=np.float64)[:, None] * BLOCK_TOKENS
    offs = np.arange(BLOCK_TOKENS, dtype=np.float64)[:, None]
    base = np.stack([np.cos(rows * freq), np.sin(rows * freq)]).astype(np.float32)
    off = np.stack([np.cos(offs * freq), np.sin(offs * freq)]).astype(np.float32)
    return base, off


def owner_kernel(
    share, pool, len_ref, q_ref, nk_ref, iv_ref, kl_ref, rk_ref, sm_ref, ch_ref, tab_ref, off_ref,
    w_ref, fresh_ref,
    lf, sc, rp, qp, qr, fs_scr, fm_scr, fw_scr, m_scr, x_scr, cnt_scr, osc,
):
    tokens, rank = kl_ref.shape
    heads, blocks = sm_ref.shape
    combos = ch_ref.shape[0]
    steps = combos // heads
    n_sel = ch_ref.shape[1]
    rows = q_ref.shape[0]
    group = rows // combos
    slots = osc.shape[2]
    keepers = slots // share
    pairs = heads // 2
    parts = lf.shape[0]
    scale = HEAD_SIZE ** -0.5
    length = len_ref[0]
    lane = lax.broadcasted_iota(jnp.int32, (1, HEAD_SIZE), 1)
    low = lane < HALF

    def widen(i, _):
        s = pl.ds(pl.multiple_of(i * blocks, blocks), blocks)
        x = kl_ref[s, :].astype(F32)
        for d in range(parts):
            y = x[:, d * HEAD_SIZE:min(rank, (d + 1) * HEAD_SIZE)]
            if y.shape[1] < HEAD_SIZE:
                y = jnp.concatenate([y, jnp.zeros((blocks, HEAD_SIZE - y.shape[1]), F32)], axis=1)
            lf[d, s, :] = y
        return _

    lax.fori_loop(0, tokens // blocks, widen, 0)

    for p in range(pairs):
        r0 = rk_ref[:, (2 * p) * HEAD_SIZE:(2 * p + 1) * HEAD_SIZE].astype(F32)
        r1 = rk_ref[:, (2 * p + 1) * HEAD_SIZE:(2 * p + 2) * HEAD_SIZE].astype(F32)
        first = jnp.where(low, r0, pltpu.roll(r1, HALF, 1))
        second = jnp.where(low, pltpu.roll(r0, HALF, 1), r1)
        both = jnp.concatenate([first, second], axis=1)
        if rp.shape[1] > rank:
            both = jnp.concatenate([both, jnp.zeros((rp.shape[1] - rank, 2 * HEAD_SIZE), F32)], axis=0)
        rp[p] = both.astype(BF16)

    sign = jnp.where(low, -1.0, 1.0).astype(F32)

    def angle(position):
        b = position // BLOCK_TOKENS
        j = position - b * BLOCK_TOKENS
        cb = tab_ref[0, pl.ds(b, 1), :]
        sb = tab_ref[1, pl.ds(b, 1), :]
        cj = off_ref[0, pl.ds(j, 1), :]
        sj = off_ref[1, pl.ds(j, 1), :]
        return cb * cj - sb * sj, (sb * cj + cb * sj) * sign

    per_step = heads * group
    fresh_keys = []
    for s in range(steps):
        c, sn = angle(length + s)
        x = q_ref[s * per_step:(s + 1) * per_step, :].astype(F32)
        x = x * c + pltpu.roll(x, HALF, 1) * sn
        qr[s * per_step:(s + 1) * per_step, :] = x.astype(BF16).astype(F32)
        y = nk_ref[s * heads:(s + 1) * heads, :].astype(F32)
        fresh_keys.append(y * c + pltpu.roll(y, HALF, 1) * sn)
    fk = jnp.concatenate(fresh_keys, axis=0).astype(BF16)
    fs = mm(qr[...].astype(BF16), fk, NT) * scale
    ri = lax.broadcasted_iota(jnp.int32, fs.shape, 0)
    ci = lax.broadcasted_iota(jnp.int32, fs.shape, 1)
    keep = jnp.logical_and((ri // group) % heads == ci % heads, ci // heads <= ri // per_step)
    fs = jnp.where(keep, fs, -jnp.inf)
    fs_scr[...] = fs
    fm_scr[...] = jnp.max(fs, axis=1, keepdims=True)

    for p in range(pairs):
        pieces = []
        for s in range(steps):
            for hh in range(2):
                start = s * per_step + (2 * p + hh) * group
                x = qr[start:start + group, :]
                y = pltpu.roll(x, HALF, 1)
                if hh == 0:
                    pieces.append(jnp.concatenate([jnp.where(low, x, 0.0), jnp.where(low, y, 0.0)], axis=1))
                else:
                    pieces.append(jnp.concatenate([jnp.where(low, 0.0, y), jnp.where(low, 0.0, x)], axis=1))
        qp[p] = jnp.concatenate(pieces, axis=0).astype(BF16)

    def keys(j, _):
        lj = jnp.concatenate(
            [lf[d, pl.ds(j, blocks, stride=BLOCK_TOKENS), :] for d in range(parts)], axis=1
        ).astype(BF16)
        cj = off_ref[0, pl.ds(j, 1), :]
        sj = off_ref[1, pl.ds(j, 1), :]
        cb = tab_ref[0, :blocks, :]
        sb = tab_ref[1, :blocks, :]
        ct = cb * cj - sb * sj
        st = sb * cj + cb * sj
        for p in range(pairs):
            raw = mm(lj, rp[p])
            a = raw[:, :HEAD_SIZE]
            c = raw[:, HEAD_SIZE:]
            k = jnp.concatenate([a * ct - c * st, c * ct + a * st], axis=1).astype(BF16)
            out = mm(qp[p], k, NT)
            for s in range(steps):
                sc[j, s * per_step + 2 * p * group:s * per_step + 2 * (p + 1) * group, :] = (
                    out[s * 2 * group:(s + 1) * 2 * group, :]
                )
        return _

    lax.fori_loop(0, BLOCK_TOKENS, keys, 0)

    block_i = lax.broadcasted_iota(jnp.int32, (blocks, n_sel), 0)
    keeper_i = lax.broadcasted_iota(jnp.int32, (keepers, blocks), 0)
    ones = jnp.ones((8, n_sel), BF16)

    def choose(c, _):
        hot = jnp.where(block_i == ch_ref[pl.ds(c, 1), :], 1.0, 0.0).astype(BF16)
        m = mm(ones, hot, NT)
        m_scr[c] = m
        kb = sm_ref[pl.ds(c % heads, 1), :] // pool
        x = jnp.where(jnp.logical_and(keeper_i == kb, m[:1] > 0.5), 1.0, 0.0)
        x_scr[pl.ds(pl.multiple_of(c * keepers, keepers), keepers), :] = x.astype(BF16)
        return _

    lax.fori_loop(0, combos, choose, 0)
    tri = jnp.where(
        lax.broadcasted_iota(jnp.int32, (blocks, blocks), 0)
        < lax.broadcasted_iota(jnp.int32, (blocks, blocks), 1), 1.0, 0.0
    ).astype(BF16)
    cnt_scr[...] = mm(x_scr[...], tri)

    slot_i = lax.broadcasted_iota(jnp.int32, (slots, blocks), 0)
    pos0 = lax.broadcasted_iota(jnp.int32, (group, blocks), 1) * BLOCK_TOKENS
    sub = lax.broadcasted_iota(jnp.int32, (group, blocks), 0)
    planes = osc.shape[0]

    def weigh(c, _):
        here = pl.ds(pl.multiple_of(c * group, group), group)
        m = m_scr[c] > 0.5
        xs = []
        for j in range(BLOCK_TOKENS):
            ok = jnp.logical_and(m, pos0 + j < length)
            xs.append(jnp.where(ok, sc[j, here, :] * scale, -jnp.inf))
        top = functools.reduce(jnp.maximum, xs)
        top = jnp.maximum(jnp.max(top, axis=1, keepdims=True), fm_scr[here, :])
        es = [jnp.exp(x - top) for x in xs]
        fe = jnp.exp(fs_scr[here, :] - top)
        total = jnp.sum(functools.reduce(jnp.add, es), axis=1, keepdims=True)
        total = total + jnp.sum(fe, axis=1, keepdims=True)
        inv = 1.0 / total
        fw_scr[here, :] = fe * inv
        slot_row = sm_ref[pl.ds(c % heads, 1), :]
        kb = slot_row // pool
        inside = slot_row - kb * pool
        hi = inside // 256
        lo = inside - hi * 256
        extra = jnp.where(sub == 0, hi, jnp.where(sub == 1, lo, 0)).astype(F32)
        lhs = jnp.concatenate([e * inv for e in es] + [extra, jnp.zeros_like(extra)], axis=0).astype(BF16)
        mine = pl.ds(pl.multiple_of(c * keepers, keepers), keepers)
        order = jnp.sum(x_scr[mine, :].astype(F32) * cnt_scr[mine, :], axis=0, keepdims=True)
        slot = jnp.where(m[:1], kb * share + order.astype(jnp.int32), -1)
        pick = jnp.where(slot_i == slot, 1.0, 0.0).astype(BF16)
        o = mm(lhs, pick, NT)
        for t in range(planes):
            osc[t, here, :] = o[t * group:(t + 1) * group, :]
        return _

    lax.fori_loop(0, combos, weigh, 0)
    fresh_ref[...] = mm(fw_scr[...].astype(BF16), iv_ref[...])

    turned = [osc[t].T for t in range(planes)]
    if share % 8 == 0:
        for k in range(keepers):
            pieces = [t[k * share:(k + 1) * share, :] for t in turned]
            rest = w_ref.shape[1] - planes * share
            if rest:
                pieces.append(jnp.zeros((rest, rows), F32))
            w_ref[k] = jnp.concatenate(pieces, axis=0).astype(BF16)
    else:
        for t in range(planes):
            w_ref[t] = turned[t].astype(BF16)


def owner(length, q, nk, iv, kl, rk, sm, ch, share, n, pool):
    tokens, rank = kl.shape
    heads, blocks = sm.shape
    combos, n_sel = ch.shape
    rows = q.shape[0]
    slots = n * share
    planes = BLOCK_TOKENS + 1
    wire = -(-planes * share // 16) * 16
    base, off = rope_tables(blocks)
    pairs = heads // 2
    direct = share % 8 == 0
    w_shape = (n, wire, rows) if direct else (planes, slots, rows)
    vmem = pl.BlockSpec(memory_space=pltpu.VMEM)
    w, fresh = pl.pallas_call(
        functools.partial(owner_kernel, share, pool),
        out_shape=(jax.ShapeDtypeStruct(w_shape, BF16), jax.ShapeDtypeStruct((rows, HEAD_SIZE), F32)),
        in_specs=[pl.BlockSpec(memory_space=pltpu.SMEM)] + [vmem] * 9,
        out_specs=(vmem, vmem),
        scratch_shapes=[
            pltpu.VMEM((-(-rank // HEAD_SIZE), tokens, HEAD_SIZE), F32),
            pltpu.VMEM((BLOCK_TOKENS, rows, blocks), F32),
            pltpu.VMEM((pairs, -(-rank // HEAD_SIZE) * HEAD_SIZE, 2 * HEAD_SIZE), BF16),
            pltpu.VMEM((pairs, rows // pairs, 2 * HEAD_SIZE), BF16),
            pltpu.VMEM((rows, HEAD_SIZE), F32),
            pltpu.VMEM((rows, nk.shape[0]), F32),
            pltpu.VMEM((rows, 1), F32),
            pltpu.VMEM((rows, nk.shape[0]), F32),
            pltpu.VMEM((combos, 8, blocks), F32),
            pltpu.VMEM((combos * n, blocks), BF16),
            pltpu.VMEM((combos * n, blocks), F32),
            pltpu.VMEM((planes, rows, slots), F32),
        ],
        compiler_params=pltpu.CompilerParams(vmem_limit_bytes=48 * 1024 * 1024),
        name="owner",
    )(length, q, nk, iv, kl, rk, sm, ch, jnp.asarray(base), jnp.asarray(off))
    if not direct:
        w = w.reshape(planes, n, share, rows).transpose(1, 0, 2, 3).reshape(n, planes * share, rows)
        w = jnp.pad(w, ((0, 0), (0, wire - planes * share), (0, 0)))
    return w, fresh


def holder_kernel(share, combos, par_ref, w_ref, v_ref, keep_ref, send_ref, vbuf, idx_v, idx_s, vsem, isem):
    n, wire, rows = w_ref.shape
    group = rows // combos
    body = BLOCK_TOKENS * share
    fuse = max(1, min(combos, 256 // body))
    load = pltpu.make_async_copy(v_ref, vbuf, vsem)
    load.start()
    raw = w_ref[:, body:body + share, :].astype(F32).reshape(n * share, rows).astype(BF16)
    ci = lax.broadcasted_iota(jnp.int32, (combos, rows), 0)
    li = lax.broadcasted_iota(jnp.int32, (combos, rows), 1)
    sel = jnp.where(li == ci * group, 256.0, jnp.where(li == ci * group + 1, 1.0, 0.0)).astype(BF16)
    idx_v[...] = mm(sel, raw, NT).astype(jnp.int32)
    fetch = pltpu.make_async_copy(idx_v, idx_s, isem)
    fetch.start()
    width = fuse * body
    a = lax.broadcasted_iota(jnp.int32, (body, width), 0)
    b = lax.broadcasted_iota(jnp.int32, (body, width), 1) % body
    turn = jnp.where(
        jnp.logical_and(a // share == b % BLOCK_TOKENS, a % share == b // BLOCK_TOKENS), 1.0, 0.0
    ).astype(BF16)
    rc = lax.broadcasted_iota(jnp.int32, (rows, width), 0) // group
    own = (rc % fuse) == lax.broadcasted_iota(jnp.int32, (rows, width), 1) // body
    fetch.wait()
    load.wait()
    par = par_ref[0]

    def one(r):
        wt = w_ref[r, :body, :].astype(F32).T.astype(BF16)
        wide = jnp.where(own, mm(wt, turn), 0.0).astype(BF16)
        outs = []
        for g in range(combos // fuse):
            tiles = []
            for c in range(fuse):
                for i in range(share):
                    tiles.append(vbuf[idx_s[g * fuse + c, r * share + i]])
            outs.append(mm(wide[g * fuse * group:(g + 1) * fuse * group, :], jnp.concatenate(tiles, axis=0)))
        return jnp.concatenate(outs, axis=0)

    def step(m, _):
        send_ref[m] = one(2 * m + 1 - par).astype(BF16)
        keep_ref[m] = one(2 * m + par)
        return _

    lax.fori_loop(0, n // 2, step, 0)


def holder(par, w, v, share, combos):
    n, wire, rows = w.shape
    vmem = pl.BlockSpec(memory_space=pltpu.VMEM)
    return pl.pallas_call(
        functools.partial(holder_kernel, share, combos),
        out_shape=(
            jax.ShapeDtypeStruct((n // 2, rows, HEAD_SIZE), F32),
            jax.ShapeDtypeStruct((n // 2, rows, HEAD_SIZE), BF16),
        ),
        in_specs=[pl.BlockSpec(memory_space=pltpu.SMEM), vmem, pl.BlockSpec(memory_space=pl.ANY)],
        out_specs=(vmem, vmem),
        scratch_shapes=[
            pltpu.VMEM(v.shape, v.dtype),
            pltpu.VMEM((combos, n * share), jnp.int32),
            pltpu.SMEM((combos, n * share), jnp.int32),
            pltpu.SemaphoreType.DMA,
            pltpu.SemaphoreType.DMA,
        ],
        compiler_params=pltpu.CompilerParams(vmem_limit_bytes=56 * 1024 * 1024),
        name="holder",
    )(par, w, v)


def per_device(
    queries, new_keys, incoming_values, key_left, right_key_factor, value_tile_store, slot_map, chosen, lengths,
):
    n = lax.axis_size("store")
    me = lax.axis_index("store")
    steps, _, heads, n_sel = chosen.shape
    blocks = slot_map.shape[2]
    combos = steps * heads
    share = max(1, blocks // n // 4)
    pool = value_tile_store.shape[0]
    q = queries.reshape(-1, HEAD_SIZE)
    w, fresh = owner(
        lengths, q, new_keys.reshape(-1, HEAD_SIZE), incoming_values.reshape(-1, HEAD_SIZE), key_left[0],
        right_key_factor[0], slot_map[0], chosen.reshape(combos, n_sel), share, n, pool,
    )
    w, store = lax.optimization_barrier((w, value_tile_store))
    tiles = store.reshape(pool, BLOCK_TOKENS, HEAD_SIZE)
    w = lax.all_to_all(w, "store", split_axis=0, concat_axis=0, tiled=True)
    par = (me % 2).astype(jnp.int32).reshape(1)
    keep, send = holder(par, w, tiles, share, combos)
    other = lax.ppermute(send, "store", [(i, i ^ 1) for i in range(n)])
    both = (keep + other.astype(F32)).astype(BF16)
    groups = [[i for i in range(n) if i % 2 == c] for c in range(2)]
    parts = lax.all_to_all(both, "store", split_axis=0, concat_axis=0, tiled=True, axis_index_groups=groups)
    out = fresh + jnp.sum(parts.astype(F32), axis=0)
    return out.astype(BF16).reshape(queries.shape)


def solution(mesh):
    in_specs = (
        P(None, ("groups", "store"), None),
        P(None, ("groups", "store"), None),
        P(None, ("groups", "store"), None),
        P(("groups", "store"), None, None),
        P(("groups", "store"), None, None),
        P(("groups", "store"), None),
        P(("groups", "store"), None, None),
        P(None, ("groups", "store"), None, None),
        P(("groups", "store")),
    )
    out_specs = P(None, ("groups", "store"), None)
    return jax.shard_map(
        per_device, mesh=mesh, in_specs=in_specs, out_specs=out_specs, check_vma=False
    )
```

time: 158 us -> 74.3 us (0.47)
  the two profiles are of different devices: /device:TPU:11 before, /device:TPU:0 now
where the time goes in v1:
time: 74.3 us; the launch traced here: 73.5 us
  Pallas kernels  28 us (38%)
  local copies, waits for them, and re-layouts  19.6 us (26%)
  blocking collectives  12.6 us (17%)
  starting transfers between devices  7.53 us (10%)
  waiting for transfers between devices  3.95 us (5%)
  other arithmetic  1.16 us (2%)
    pallas_call x1, Pallas kernels, owner(): pl.pallas_call(functools.partial(owner_kernel, share, pool), out_shape=(j...  18.1 us
    unnamed x14, local copies, waits for them, and re-layouts  16.8 us
    all_to_all x1, blocking collectives, per_device(): lax.all_to_all(both, 'store', split_axis=0, concat_axis=0, tiled=True, ax...  12.6 us
    pallas_call x1, Pallas kernels, holder(): pl.pallas_call(functools.partial(holder_kernel, share, combos), out_shape...  9.92 us
    all_to_all x1, starting transfers between devices, per_device(): w = lax.all_to_all(w, 'store', split_axis=0, concat_axis=0, tiled=True)  7.36 us
    all_to_all x1, waiting for transfers between devices, per_device(): w = lax.all_to_all(w, 'store', split_axis=0, concat_axis=0, tiled=True)  2.31 us
    ppermute x1, waiting for transfers between devices, per_device(): other = lax.ppermute(send, 'store', [(i, i ^ 1) for i in range(n)])  1.64 us
  transfers between devices with their start and end apart: 2, of which 2 were waited for; matrix products, arithmetic and copies ran while one was open for 12% of the time, Pallas kernels for 0%

profile of v1, /device:TPU:0, one launch (start us, length us, event | category | flops | bytes accessed | tf_op | source)
XLA Modules:
  0.0 73.5 jit_solution(17161055589642772240)
XLA Ops:
  0.7 0.7 reshape.22.nk_ref
  1.4 0.7 reshape.23.iv_ref
  2.0 0.8 %reshape.21.q_ref = bf16[128,128]{1,0:T(8,128)(2,1)S(1)} reshape(bf16[2,1,8192]{2,0,1:T(2,128)(2,1)} %param.11) | data formatting | bytes 65536 | tf_op jit(solution)/shard_map/reshape | solution.py:337
  2.8 3.1 %copy.12 = bf16[1,4096,160]{2,1,0:T(8,128)(2,1)S(1)} copy(bf16[1,4096,160]{1,2,0:T(8,128)(2,1)} %param.14) | data formatting | bytes 2621440 | tf_op args[3]
  5.9 0.0 copy-start
  6.0 1.0 %copy-done = f32[2,520,128]{2,1,0:T(8,128)S(1)} copy-done((f32[2,520,128]{2,1,0:T(8,128)S(1)}, f32[2,520,128]{2,1,0:T(8,128)}, u32[]{:S(2)}) %copy-start) | copy-done | bytes 532504
  7.0 0.0 copy-start.1
  7.0 1.0 %copy-done.1 = bf16[1,160,1024]{2,1,0:T(8,128)(2,1)S(1)} copy-done((bf16[1,160,1024]{2,1,0:T(8,128)(2,1)S(1)}, bf16[1,160,1024]{2,1,0:T(8,128)(2,1)}, u32[]{:S(2)}) %copy-start.1) | copy-done | bytes 327704
  8.0 0.0 copy-start.2
  8.0 0.7 copy-done.2
  8.7 0.0 copy-start.3
  8.7 0.7 copy-done.3
  9.4 0.0 copy-start.4
  9.4 0.7 copy-done.4
  10.1 18.1 %owner.1 = (bf16[16,80,128]{2,1,0:T(8,128)(2,1)}, f32[128,128]{1,0:T(8,128)S(1)}) custom-call(s32[1]{0:T(128)S(6)} %copy.14.len_ref, bf16[128,128]{1,0:T(8,128)(2,1)S(1)} %reshape.21.q_ref, bf16[16,128]{1,0:T(8,128)(2,1)S(1)} %reshape.22.nk_ref, bf16[16,128]{1,0:T(8,128)(2,1)S(1)} %reshape.23.iv_ref, bf16[4096,160]{1,0:T(8,128)(2,1)S(1)} %bitcast.13, ...), custom_call_target="tpu_custom_call" | custom-call | tf_op jit(solution)/shard_map/owner/pallas_call | solution.py:230
  28.1 7.4 %all-to-all-start = ((bf16[16,80,128]{2,1,0:T(8,128)(2,1)}), bf16[16,80,128]{2,1,0:T(8,128)(2,1)S(1)}, u32[]{:S(2)}, u32[]{:S(2)}) async-start(bf16[16,80,128]{2,1,0:T(8,128)(2,1)} %get-tuple-element.13), calls=%async_computation | async-start | bytes 655360 | tf_op jit(solution)/shard_map/all_to_all | solution.py:344
  35.5 8.8 %copy.13 = bf16[512,8,8,128]{3,2,1,0:T(8,128)(2,1)} copy(bf16[512,8,8,128]{3,1,2,0:T(8,128)(2,1)} %bitcast.18) | data formatting | bytes 16777216
  44.3 2.3 %all-to-all-done.w_ref = bf16[16,80,128]{2,1,0:T(8,128)(2,1)S(1)} async-done(((bf16[16,80,128]{2,1,0:T(8,128)(2,1)}), bf16[16,80,128]{2,1,0:T(8,128)(2,1)S(1)}, u32[]{:S(2)}, u32[]{:S(2)}) %all-to-all-start) | async-done | bytes 327712 | tf_op jit(solution)/shard_map/all_to_all | solution.py:344
  46.6 0.0 copy-start.5
  46.6 0.8 %copy-done.5 = bf16[16,80,128]{2,1,0:T(8,128)(2,1)} copy-done((bf16[16,80,128]{2,1,0:T(8,128)(2,1)}, bf16[16,80,128]{2,1,0:T(8,128)(2,1)S(1)}, u32[]{:S(2)}) %copy-start.5) | copy-done | bytes 327704
  47.3 9.9 %holder.1 = (f32[8,128,128]{2,1,0:T(8,128)}, bf16[8,128,128]{2,1,0:T(8,128)(2,1)}) custom-call(s32[1]{0:T(128)} %bitcast.4.par_ref, bf16[16,80,128]{2,1,0:T(8,128)(2,1)} %copy-done.5, bf16[4096,8,128]{2,1,0:T(8,128)(2,1)} %bitcast.17), custom_call_target="tpu_custom_call" | custom-call | tf_op jit(solution)/shard_map/holder/pallas_call | solution.py:307
  57.3 0.2 collective-permute-start
  57.5 1.6 %collective-permute-done = bf16[8,128,128]{2,1,0:T(8,128)(2,1)S(1)} collective-permute-done((bf16[8,128,128]{2,1,0:T(8,128)(2,1)}, bf16[8,128,128]{2,1,0:T(8,128)(2,1)S(1)}, u32[]{:S(2)}, u32[]{:S(2)}) %collective-permute-start) | collective-permute-done | bytes 262176 | tf_op jit(solution)/shard_map/ppermute | solution.py:347
  59.1 1.1 %add_convert_fusion = bf16[8,128,128]{2,1,0:T(8,128)(2,1)S(1)} fusion(f32[8,128,128]{2,1,0:T(8,128)} %get-tuple-element.15, bf16[8,128,128]{2,1,0:T(8,128)(2,1)S(1)} %collective-permute-done), kind=kLoop, calls=%fused_computation.1 | loop fusion | flops 393216 | bytes 1048576 | tf_op jit(solution)/shard_map/convert_element_type | solution.py:348
  60.2 12.6 %all_to_all.10 = bf16[8,128,128]{2,1,0:T(8,128)(2,1)S(1)} all-to-all(bf16[8,128,128]{2,1,0:T(8,128)(2,1)S(1)} %add_convert_fusion), channel_id=1, replica_groups={{0,2,4,6,8,10,12,14},{1,3,5,7,9,11,13,15},{16,18,20,22,24,26,28,30},{17..., dimensions={0} | all-to-all | bytes 524288 | tf_op jit(solution)/shard_map/all_to_all | solution.py:350
  72.9 0.6 reshape.27
  (2 shorter events, 0.0 us)
Async XLA Ops:
  5.9 1.0 %copy-start = (f32[2,520,128]{2,1,0:T(8,128)S(1)}, f32[2,520,128]{2,1,0:T(8,128)}, u32[]{:S(2)}) copy-start(f32[2,520,128]{2,1,0:T(8,128)} %constant.23.clone.tab_ref) | copy-start | bytes 1597444
  7.0 1.0 %copy-start.1 = (bf16[1,160,1024]{2,1,0:T(8,128)(2,1)S(1)}, bf16[1,160,1024]{2,1,0:T(8,128)(2,1)}, u32[]{:S(2)}) copy-start(bf16[1,160,1024]{2,1,0:T(8,128)(2,1)} %param.15) | copy-start | bytes 983044
  8.0 0.7 copy-start.2
  8.7 0.7 copy-start.3
  9.4 0.7 copy-start.4
  28.1 18.5 %all-to-all-start = ((bf16[16,80,128]{2,1,0:T(8,128)(2,1)}), bf16[16,80,128]{2,1,0:T(8,128)(2,1)S(1)}, u32[]{:S(2)}, u32[]{:S(2)}) async-start(bf16[16,80,128]{2,1,0:T(8,128)(2,1)} %get-tuple-element.13), calls=%async_computation | async-start | bytes 655360 | tf_op jit(solution)/shard_map/all_to_all | solution.py:344
  46.6 0.8 %copy-start.5 = (bf16[16,80,128]{2,1,0:T(8,128)(2,1)}, bf16[16,80,128]{2,1,0:T(8,128)(2,1)S(1)}, u32[]{:S(2)}) copy-start(bf16[16,80,128]{2,1,0:T(8,128)(2,1)S(1)} %all-to-all-done.w_ref) | copy-start | bytes 983044
  57.3 1.8 %collective-permute-start = (bf16[8,128,128]{2,1,0:T(8,128)(2,1)}, bf16[8,128,128]{2,1,0:T(8,128)(2,1)S(1)}, u32[]{:S(2)}, u32[]{:S(2)}) collective-permute-start(bf16[8,128,128]{2,1,0:T(8,128)(2,1)} %get-tuple-element.16), channel_id=1, source_target_pairs={{0,1},{1,0},{2,3},{3,2},{4,5},{5,4},{6,7},{7,6},{8,9},{9,8},{10,11... | collective-permute-start | bytes 786440 | tf_op jit(solution)/shard_map/ppermute | solution.py:347

commit v2 on v1

v2 whole, which is shorter than its diff:
```python
import functools

import jax
import jax.numpy as jnp
import numpy as np
from jax import lax
from jax.experimental import pallas as pl
from jax.experimental.pallas import tpu as pltpu
from jax.sharding import PartitionSpec as P

HEAD_SIZE = 128
HALF = HEAD_SIZE // 2
BLOCK_TOKENS = 8
LANES = 128
ROPE_BASE = 500000.0
NT = (((1,), (1,)), ((), ()))
NN = (((1,), (0,)), ((), ()))
F32 = jnp.float32
BF16 = jnp.bfloat16


def mm(a, b, dims=NN):
    return lax.dot_general(a, b, dims, preferred_element_type=F32)


def rope_tables(blocks):
    exponent = -(np.arange(HALF, dtype=np.float32) * np.float32(2.0) / np.float32(HEAD_SIZE))
    freq = np.float32(ROPE_BASE) ** exponent
    pos = np.arange(blocks * BLOCK_TOKENS).reshape(-1, LANES, BLOCK_TOKENS).transpose(0, 2, 1)
    pos = pos.reshape(-1, 2 * LANES).astype(np.float32)
    angle = (pos[:, None, :] * freq[None, :, None]).astype(np.float64)
    keys = np.stack([np.cos(angle), np.sin(angle)], axis=1).astype(np.float32)
    freq = np.concatenate([freq, freq]).astype(np.float64)
    rows = np.arange(-(-(blocks + 2) // 8) * 8, dtype=np.float64)[:, None] * BLOCK_TOKENS
    offs = np.arange(BLOCK_TOKENS, dtype=np.float64)[:, None]
    base = np.stack([np.cos(rows * freq), np.sin(rows * freq)]).astype(np.float32)
    off = np.stack([np.cos(offs * freq), np.sin(offs * freq)]).astype(np.float32)
    return keys, base, off


def split3(x):
    a = x.astype(BF16)
    r = x - a.astype(F32)
    b = r.astype(BF16)
    return a, b, (r - b.astype(F32)).astype(BF16)


def owner_kernel(
    share, pool, keepers, len_ref, q_hbm, nk_hbm, iv_hbm, kl_hbm, rk_hbm, sm_hbm, ch_hbm, tab_hbm, base_hbm, off_hbm,
    w_ref, fresh_ref,
    q_ref, nk_ref, iv_ref, kl_ref, rk_ref, sm_ref, ch_ref, tab_ref, base_ref, off_ref, sems,
    lp, kk, rt, qp, qr, nr, vr, sc, fs_scr, fm_scr, fw_scr, pm, osc,
):
    rank, tokens = kl_ref.shape
    heads, blocks = sm_ref.shape
    combos, n_sel = ch_ref.shape
    steps = combos // heads
    rows = qr.shape[0]
    group = rows // combos
    planes = osc.shape[0]
    slots = osc.shape[2]
    pairs = heads // 2
    per_step = heads * group
    chunks = blocks // LANES
    scale = HEAD_SIZE ** -0.5
    length = len_ref[0]

    moves = []
    for i, (src, dst) in enumerate((
        (kl_hbm, kl_ref), (rk_hbm, rk_ref), (q_hbm, q_ref), (nk_hbm, nk_ref), (iv_hbm, iv_ref), (sm_hbm, sm_ref),
        (ch_hbm, ch_ref), (base_hbm, base_ref), (off_hbm, off_ref), (tab_hbm, tab_ref),
    )):
        move = pltpu.make_async_copy(src, dst, sems.at[i])
        move.start()
        moves.append(move)

    lane = lax.broadcasted_iota(jnp.int32, (1, HEAD_SIZE), 1)
    low = lane < HALF
    half = 4 * LANES
    to = lax.broadcasted_iota(jnp.int32, (1, half), 1)
    pm[...] = jnp.where(
        lax.broadcasted_iota(jnp.int32, (half, half), 0) == (to % HALF) * BLOCK_TOKENS + to // HALF, 1.0, 0.0
    ).astype(BF16)

    for move in moves[:2]:
        move.wait()

    def order(i, _):
        at = pl.multiple_of(i * 2 * half, 2 * half)
        a = mm(kl_ref[:, pl.ds(at, half)], pm[...])
        b = mm(kl_ref[:, pl.ds(at + half, half)], pm[...])
        for m in range(BLOCK_TOKENS // 2):
            x = a[:, m * LANES:(m + 1) * LANES]
            y = b[:, m * LANES:(m + 1) * LANES]
            even = jnp.where(low, x, pltpu.roll(y, HALF, 1))
            odd = jnp.where(low, pltpu.roll(x, HALF, 1), y)
            lp[i * (BLOCK_TOKENS // 2) + m] = jnp.concatenate([even, odd], axis=1).astype(BF16)
        return _

    lax.fori_loop(0, chunks, order, 0)
    for h in range(heads):
        rt[h * HEAD_SIZE:(h + 1) * HEAD_SIZE, :] = (
            rk_ref[:, h * HEAD_SIZE:(h + 1) * HEAD_SIZE].astype(F32).T.astype(BF16)
        )

    for move in moves[2:9]:
        move.wait()
    x = q_ref[...].astype(F32)
    for k in range(per_step):
        qr[pl.ds(k, steps, stride=per_step), :] = x[:, k * HEAD_SIZE:(k + 1) * HEAD_SIZE]
    x = nk_ref[...].astype(F32)
    y = iv_ref[...].astype(F32)
    for k in range(heads):
        nr[pl.ds(k, steps, stride=heads), :] = x[:, k * HEAD_SIZE:(k + 1) * HEAD_SIZE]
        vr[pl.ds(k, steps, stride=heads), :] = y[:, k * HEAD_SIZE:(k + 1) * HEAD_SIZE]

    sign = jnp.where(low, -1.0, 1.0).astype(F32)

    def angle(position):
        b = position // BLOCK_TOKENS
        j = position - b * BLOCK_TOKENS
        cb = base_ref[0, pl.ds(b, 1), :]
        sb = base_ref[1, pl.ds(b, 1), :]
        cj = off_ref[0, pl.ds(j, 1), :]
        sj = off_ref[1, pl.ds(j, 1), :]
        return cb * cj - sb * sj, (sb * cj + cb * sj) * sign

    fresh_keys = []
    for s in range(steps):
        c, sn = angle(length + s)
        x = qr[s * per_step:(s + 1) * per_step, :]
        x = x * c + pltpu.roll(x, HALF, 1) * sn
        qr[s * per_step:(s + 1) * per_step, :] = x.astype(BF16).astype(F32)
        y = nr[s * heads:(s + 1) * heads, :]
        fresh_keys.append(y * c + pltpu.roll(y, HALF, 1) * sn)
    fk = jnp.concatenate(fresh_keys, axis=0).astype(BF16)
    fs = mm(qr[...].astype(BF16), fk, NT) * scale
    ri = lax.broadcasted_iota(jnp.int32, fs.shape, 0)
    ci = lax.broadcasted_iota(jnp.int32, fs.shape, 1)
    keep = jnp.logical_and((ri // group) % heads == ci % heads, ci // heads <= ri // per_step)
    fs = jnp.where(keep, fs, -jnp.inf)
    fs_scr[...] = fs
    fm_scr[...] = jnp.max(fs, axis=1, keepdims=True)

    for p in range(pairs):
        pieces = []
        for s in range(steps):
            for hh in range(2):
                start = s * per_step + (2 * p + hh) * group
                x = qr[start:start + group, :]
                z = jnp.zeros_like(x)
                pieces.append(jnp.concatenate([x, z] if hh == 0 else [z, x], axis=1))
        qp[p] = jnp.concatenate(pieces, axis=0).astype(BF16)

    moves[9].wait()

    def keys(i, _):
        ct = tab_ref[i, 0]
        st = tab_ref[i, 1]
        raw = mm(rt[...], lp[i])
        for h in range(heads):
            a = raw[h * HEAD_SIZE:h * HEAD_SIZE + HALF, :]
            c = raw[h * HEAD_SIZE + HALF:(h + 1) * HEAD_SIZE, :]
            kk[i, h * HEAD_SIZE:(h + 1) * HEAD_SIZE, :] = jnp.concatenate(
                [a * ct - c * st, c * ct + a * st], axis=0
            ).astype(BF16)
        return _

    lax.fori_loop(0, lp.shape[0], keys, 0, unroll=4)

    def scores(i, _):
        at = i // (BLOCK_TOKENS // 2)
        j = 2 * (i % (BLOCK_TOKENS // 2))
        for p in range(pairs):
            out = mm(qp[p], kk[i, 2 * p * HEAD_SIZE:2 * (p + 1) * HEAD_SIZE, :]) * scale
            for s in range(steps):
                to_rows = slice(s * per_step + 2 * p * group, s * per_step + 2 * (p + 1) * group)
                for jj in range(2):
                    sc[at, j + jj, to_rows, :] = out[s * 2 * group:(s + 1) * 2 * group, jj * LANES:(jj + 1) * LANES]
        return _

    lax.fori_loop(0, lp.shape[0], scores, 0, unroll=4)

    wide = steps * n_sel
    entry = lax.broadcasted_iota(jnp.int32, (1, wide), 1)
    block_i = lax.broadcasted_iota(jnp.int32, (blocks, wide), 0)
    keeper_i = lax.broadcasted_iota(jnp.int32, (keepers, wide), 0)
    slot_i = lax.broadcasted_iota(jnp.int32, (steps * slots, wide), 0)
    e0 = lax.broadcasted_iota(jnp.int32, (wide, wide), 0)
    e1 = lax.broadcasted_iota(jnp.int32, (wide, wide), 1)
    before = jnp.where(jnp.logical_and(e0 // n_sel == e1 // n_sel, e0 < e1), 1.0, 0.0).astype(BF16)
    sub = lax.broadcasted_iota(jnp.int32, (16, blocks), 0)
    sub_e = lax.broadcasted_iota(jnp.int32, (8, wide), 0)

    def weigh(h, _):
        picked = jnp.concatenate([ch_ref[pl.ds(s * heads + h, 1), :] for s in range(steps)], axis=1)
        hot = jnp.where(block_i == picked, 1.0, 0.0).astype(BF16)
        row = sm_ref[pl.ds(h, 1), :]
        kb = row // pool
        inside = row - kb * pool
        hi = inside // 256
        lo = inside - hi * 256
        extra = jnp.where(sub == 0, hi, jnp.where(sub == 1, lo, jnp.where(sub == 2, kb, 0))).astype(F32).astype(BF16)
        got = mm(extra, hot)
        kb = got[2:3, :].astype(jnp.int32)
        kh = jnp.where(keeper_i == kb, 1.0, 0.0)
        rank_e = jnp.sum(kh * mm(kh.astype(BF16), before), axis=0, keepdims=True)
        slot = kb * share + rank_e.astype(jnp.int32) + (entry // n_sel) * slots
        pick = jnp.where(slot_i == slot, 1.0, 0.0).astype(BF16)
        xs = None
        heres = []
        for s in range(steps):
            here = pl.ds(pl.multiple_of((s * heads + h) * group, group), group)
            heres.append(here)
            x = jnp.concatenate(
                [jnp.concatenate([sc[t, j, here, :] for t in range(chunks)], axis=1) for j in range(BLOCK_TOKENS)],
                axis=0,
            )
            g = mm(jnp.concatenate(split3(x), axis=0), hot)
            size = BLOCK_TOKENS * group
            g = (g[:size] + g[size:2 * size]) + g[2 * size:]
            xs = g if xs is None else jnp.where(entry // n_sel == s, g, xs)
        pos = picked * BLOCK_TOKENS
        xs = [
            jnp.where(pos + j < length, xs[j * group:(j + 1) * group, :], -jnp.inf) for j in range(BLOCK_TOKENS)
        ]
        most = functools.reduce(jnp.maximum, xs)
        tops = []
        top = None
        for s in range(steps):
            mine = entry // n_sel == s
            t = jnp.max(jnp.where(mine, most, -jnp.inf), axis=1, keepdims=True)
            t = jnp.maximum(t, fm_scr[heres[s], :])
            tops.append(t)
            top = jnp.broadcast_to(t, most.shape) if top is None else jnp.where(mine, t, top)
        es = [jnp.exp(x - top) for x in xs]
        added = functools.reduce(jnp.add, es)
        inv = None
        for s in range(steps):
            mine = entry // n_sel == s
            fe = jnp.exp(fs_scr[heres[s], :] - tops[s])
            total = jnp.sum(jnp.where(mine, added, 0.0), axis=1, keepdims=True)
            one = 1.0 / (total + jnp.sum(fe, axis=1, keepdims=True))
            fw_scr[heres[s], :] = fe * one
            inv = jnp.broadcast_to(one, most.shape) if inv is None else jnp.where(mine, one, inv)
        tail = jnp.where(sub_e < 2, got[:8, :], 0.0)
        lhs = jnp.concatenate([e * inv for e in es] + [tail, jnp.zeros_like(tail)], axis=0).astype(BF16)
        o = mm(lhs, pick, NT)
        for t in range(planes):
            for s in range(steps):
                osc[t, heres[s], :] = o[t * group:(t + 1) * group, s * slots:(s + 1) * slots]
        return _

    lax.fori_loop(0, heads, weigh, 0, unroll=2)
    fresh_ref[...] = mm(fw_scr[...].astype(BF16), vr[...].astype(BF16))

    turned = [osc[t].T for t in range(planes)]
    if share % 8 == 0:
        for k in range(keepers):
            w_ref[k] = jnp.concatenate([t[k * share:(k + 1) * share, :] for t in turned], axis=0).astype(BF16)
    else:
        for t in range(planes):
            w_ref[t] = turned[t].astype(BF16)


def owner(length, q, nk, iv, kl, rk, sm, ch, share, n, pool):
    rank, tokens = kl.shape
    heads, blocks = sm.shape
    combos, n_sel = ch.shape
    rows = q.size // HEAD_SIZE
    fresh_rows = nk.size // HEAD_SIZE
    slots = n * share
    planes = BLOCK_TOKENS + 1
    pairs = heads // 2
    direct = share % 8 == 0
    w_shape = (n, planes * share, rows) if direct else (planes, slots, rows)
    hbm = pl.BlockSpec(memory_space=pl.ANY)
    vmem = pl.BlockSpec(memory_space=pltpu.VMEM)
    operands = (q, nk, iv, kl, rk, sm, ch) + tuple(jnp.asarray(t) for t in rope_tables(blocks))
    w, fresh = pl.pallas_call(
        functools.partial(owner_kernel, share, pool, n),
        out_shape=(jax.ShapeDtypeStruct(w_shape, BF16), jax.ShapeDtypeStruct((rows, HEAD_SIZE), F32)),
        in_specs=[pl.BlockSpec(memory_space=pltpu.SMEM)] + [hbm] * len(operands),
        out_specs=(vmem, vmem),
        scratch_shapes=[pltpu.VMEM(x.shape, x.dtype) for x in operands] + [
            pltpu.SemaphoreType.DMA((len(operands),)),
            pltpu.VMEM((tokens // (2 * LANES), rank, 2 * LANES), BF16),
            pltpu.VMEM((tokens // (2 * LANES), heads * HEAD_SIZE, 2 * LANES), BF16),
            pltpu.VMEM((heads * HEAD_SIZE, rank), BF16),
            pltpu.VMEM((pairs, rows // pairs, 2 * HEAD_SIZE), BF16),
            pltpu.VMEM((rows, HEAD_SIZE), F32),
            pltpu.VMEM((fresh_rows, HEAD_SIZE), F32),
            pltpu.VMEM((fresh_rows, HEAD_SIZE), F32),
            pltpu.VMEM((blocks // LANES, BLOCK_TOKENS, rows, LANES), F32),
            pltpu.VMEM((rows, fresh_rows), F32),
            pltpu.VMEM((rows, 1), F32),
            pltpu.VMEM((rows, fresh_rows), F32),
            pltpu.VMEM((4 * LANES, 4 * LANES), BF16),
            pltpu.VMEM((planes, rows, slots), F32),
        ],
        compiler_params=pltpu.CompilerParams(vmem_limit_bytes=60 * 1024 * 1024),
        name="owner",
    )(length, *operands)
    if not direct:
        w = w.reshape(planes, n, share, rows).transpose(1, 0, 2, 3).reshape(n, planes * share, rows)
    return w, fresh


def holder_kernel(share, combos, par_ref, w_ref, v_ref, keep_ref, send_ref, idx_v, idx_s, isem):
    n, wire, rows = w_ref.shape
    group = rows // combos
    body = BLOCK_TOKENS * share
    fuse = max(1, min(combos, 256 // body))
    raw = w_ref[:, body:body + share, :].astype(F32).reshape(n * share, rows).astype(BF16)
    ci = lax.broadcasted_iota(jnp.int32, (combos, rows), 0)
    li = lax.broadcasted_iota(jnp.int32, (combos, rows), 1)
    sel = jnp.where(li == ci * group, 256.0, jnp.where(li == ci * group + 1, 1.0, 0.0)).astype(BF16)
    idx_v[...] = mm(sel, raw, NT).astype(jnp.int32)
    fetch = pltpu.make_async_copy(idx_v, idx_s, isem)
    fetch.start()
    width = fuse * body
    a = lax.broadcasted_iota(jnp.int32, (body, width), 0)
    b = lax.broadcasted_iota(jnp.int32, (body, width), 1) % body
    turn = jnp.where(
        jnp.logical_and(a // share == b % BLOCK_TOKENS, a % share == b // BLOCK_TOKENS), 1.0, 0.0
    ).astype(BF16)
    rc = lax.broadcasted_iota(jnp.int32, (rows, width), 0) // group
    own = (rc % fuse) == lax.broadcasted_iota(jnp.int32, (rows, width), 1) // body
    fetch.wait()
    par = par_ref[0]

    def one(r):
        wt = w_ref[r, :body, :].astype(F32).T.astype(BF16)
        wide = jnp.where(own, mm(wt, turn), 0.0).astype(BF16)
        outs = []
        for g in range(combos // fuse):
            tiles = []
            for c in range(fuse):
                for i in range(share):
                    tiles.append(v_ref[idx_s[g * fuse + c, r * share + i]])
            outs.append(mm(wide[g * fuse * group:(g + 1) * fuse * group, :], jnp.concatenate(tiles, axis=0)))
        return jnp.concatenate(outs, axis=0)

    def step(m, _):
        send_ref[m] = one(2 * m + 1 - par).astype(BF16)
        keep_ref[m] = one(2 * m + par)
        return _

    lax.fori_loop(0, n // 2, step, 0)


def holder(par, w, v, share, combos):
    n, wire, rows = w.shape
    vmem = pl.BlockSpec(memory_space=pltpu.VMEM)
    return pl.pallas_call(
        functools.partial(holder_kernel, share, combos),
        out_shape=(
            jax.ShapeDtypeStruct((n // 2, rows, HEAD_SIZE), F32),
            jax.ShapeDtypeStruct((n // 2, rows, HEAD_SIZE), BF16),
        ),
        in_specs=[pl.BlockSpec(memory_space=pltpu.SMEM), vmem, vmem],
        out_specs=(vmem, vmem),
        scratch_shapes=[
            pltpu.VMEM((combos, n * share), jnp.int32),
            pltpu.SMEM((combos, n * share), jnp.int32),
            pltpu.SemaphoreType.DMA,
        ],
        compiler_params=pltpu.CompilerParams(vmem_limit_bytes=20 * 1024 * 1024),
        name="holder",
    )(par, w, v)


def per_device(
    queries, new_keys, incoming_values, key_left, right_key_factor, value_tile_store, slot_map, chosen, lengths,
):
    n = lax.axis_size("store")
    me = lax.axis_index("store")
    steps, _, heads, n_sel = chosen.shape
    blocks = slot_map.shape[2]
    combos = steps * heads
    share = max(1, blocks // n // 4)
    pool = value_tile_store.shape[0]
    w, fresh = owner(
        lengths, queries[:, 0], new_keys[:, 0], incoming_values[:, 0], key_left[0].T,
        right_key_factor[0], slot_map[0], chosen.reshape(combos, n_sel), share, n, pool,
    )
    w, store = lax.optimization_barrier((w, value_tile_store))
    tiles = store.reshape(pool, BLOCK_TOKENS, HEAD_SIZE)
    w = lax.all_to_all(w, "store", split_axis=0, concat_axis=0, tiled=True)
    par = (me % 2).astype(jnp.int32).reshape(1)
    keep, send = holder(par, w, tiles, share, combos)
    other = lax.ppermute(send, "store", [(i, i ^ 1) for i in range(n)])
    both = (keep + other.astype(F32)).astype(BF16)
    groups = [[i for i in range(n) if i % 2 == c] for c in range(2)]
    parts = lax.all_to_all(both, "store", split_axis=0, concat_axis=0, tiled=True, axis_index_groups=groups)
    out = fresh + jnp.sum(parts.astype(F32), axis=0)
    return out.astype(BF16).reshape(queries.shape)


def solution(mesh):
    in_specs = (
        P(None, ("groups", "store"), None),
        P(None, ("groups", "store"), None),
        P(None, ("groups", "store"), None),
        P(("groups", "store"), None, None),
        P(("groups", "store"), None, None),
        P(("groups", "store"), None),
        P(("groups", "store"), None, None),
        P(None, ("groups", "store"), None, None),
        P(("groups", "store")),
    )
    out_specs = P(None, ("groups", "store"), None)
    return jax.shard_map(
        per_device, mesh=mesh, in_specs=in_specs, out_specs=out_specs, check_vma=False
    )
```

time: 74.3 us -> 59.3 us (0.80)
  local copies, waits for them, and re-layouts: 19.6 us -> 12.8 us
  Pallas kernels: 28 us -> 21.4 us
  other arithmetic: 1.16 us -> 0.11 us
    unnamed x14 -> x5, local copies, waits for them, and re-layouts: 16.8 us -> 12.2 us
    pallas_call x1, Pallas kernels: 9.92 us -> 5.56 us  [holder(): pl.pallas_call(functools.partial(holder_kernel, share, combos), out_shape...]
    reshape x3 -> x0, local copies, waits for them, and re-layouts: 2.19 us -> none  [the longest x1 0.79 us: per_device(): q = queries.reshape(-1, HEAD_SIZE)]
    pallas_call x1, Pallas kernels: 18.1 us -> 15.9 us  [owner(): pl.pallas_call(functools.partial(owner_kernel, share, pool, n), out_shape...]
    convert_element_type x1, other arithmetic: 1.11 us -> 0.06 us  [per_device(): both = (keep + other.astype(F32)).astype(BF16)]
  transfers between devices with their start and end apart: 2 -> 2, of which waited for: 2 -> 2; matrix products, arithmetic and copies ran while one was open for 12% -> 15% of each run, Pallas kernels for 0% -> 0%
where the time goes in v2:
time: 59.3 us; the launch traced here: 59 us
  Pallas kernels  21.4 us (36%)
  blocking collectives  13.2 us (22%)
  local copies, waits for them, and re-layouts  12.8 us (22%)
  starting transfers between devices  7.44 us (13%)
  waiting for transfers between devices  3.28 us (6%)
  between operations  0.72 us (1%)
    pallas_call x1, Pallas kernels, owner(): pl.pallas_call(functools.partial(owner_kernel, share, pool, n), out_shape...  15.9 us
    all_to_all x1, blocking collectives, per_device(): lax.all_to_all(both, 'store', split_axis=0, concat_axis=0, tiled=True, ax...  13.2 us
    unnamed x5, local copies, waits for them, and re-layouts  12.2 us
    all_to_all x1, starting transfers between devices, per_device(): w = lax.all_to_all(w, 'store', split_axis=0, concat_axis=0, tiled=True)  7.37 us
    pallas_call x1, Pallas kernels, holder(): pl.pallas_call(functools.partial(holder_kernel, share, combos), out_shape...  5.56 us
    all_to_all x1, waiting for transfers between devices, per_device(): w = lax.all_to_all(w, 'store', split_axis=0, concat_axis=0, tiled=True)  1.76 us
    ppermute x1, waiting for transfers between devices, per_device(): other = lax.ppermute(send, 'store', [(i, i ^ 1) for i in range(n)])  1.52 us
  transfers between devices with their start and end apart: 2, of which 2 were waited for; matrix products, arithmetic and copies ran while one was open for 15% of the time, Pallas kernels for 0%

profile of v2, /device:TPU:0, one launch (start us, length us, event | category | flops | bytes accessed | tf_op | source)
XLA Modules:
  0.0 59.0 jit_solution(2756380967233119973)
XLA Ops:
  0.7 15.9 %owner.1 = (bf16[16,72,128]{2,1,0:T(8,128)(2,1)}, f32[128,128]{1,0:T(8,128)}) custom-call(s32[1]{0:T(128)S(6)} %copy.14.len_ref, bf16[2,8192]{1,0:T(2,128)(2,1)} %bitcast.16, bf16[2,1024]{1,0:T(2,128)(2,1)} %bitcast.19, bf16[2,1024]{1,0:T(2,128)(2,1)} %bitcast.20, bf16[160,4096]{1,0:T(8,128)(2,1)} %bitcast.14, bf16[160,1024]{1,0:T(8,128)(2,1)} %bitcast.15, ...), custom_call_target="tpu_custom_call" | custom-call | tf_op jit(solution)/shard_map/owner/pallas_call | solution.py:280
  16.5 7.4 %all-to-all-start = ((bf16[16,72,128]{2,1,0:T(8,128)(2,1)}), bf16[16,72,128]{2,1,0:T(8,128)(2,1)S(1)}, u32[]{:S(2)}, u32[]{:S(2)}) async-start(bf16[16,72,128]{2,1,0:T(8,128)(2,1)} %get-tuple-element.13), calls=%async_computation | async-start | bytes 589824 | tf_op jit(solution)/shard_map/all_to_all | solution.py:389
  23.9 0.0 copy-start.1
  23.9 8.8 %copy.13 = bf16[512,8,8,128]{3,2,1,0:T(8,128)(2,1)} copy(bf16[512,8,8,128]{3,1,2,0:T(8,128)(2,1)} %bitcast.13) | data formatting | bytes 16777216
  32.7 1.8 %all-to-all-done.w_ref = bf16[16,72,128]{2,1,0:T(8,128)(2,1)S(1)} async-done(((bf16[16,72,128]{2,1,0:T(8,128)(2,1)}), bf16[16,72,128]{2,1,0:T(8,128)(2,1)S(1)}, u32[]{:S(2)}, u32[]{:S(2)}) %all-to-all-start) | async-done | bytes 294944 | tf_op jit(solution)/shard_map/all_to_all | solution.py:389
  34.5 0.0 copy-start
  34.5 3.4 %copy-done = bf16[512,8,8,128]{3,2,1,0:T(8,128)(2,1)S(1)} copy-done((bf16[512,8,8,128]{3,2,1,0:T(8,128)(2,1)S(1)}, bf16[512,8,8,128]{3,2,1,0:T(8,128)(2,1)}, u32[]{:S(2)}) %copy-start) | copy-done | bytes 8388632
  37.9 5.6 %holder.1 = (f32[8,128,128]{2,1,0:T(8,128)S(1)}, bf16[8,128,128]{2,1,0:T(8,128)(2,1)S(1)}) custom-call(s32[1]{0:T(128)} %bitcast.8.par_ref, bf16[16,72,128]{2,1,0:T(8,128)(2,1)S(1)} %all-to-all-done.w_ref, bf16[4096,8,128]{2,1,0:T(8,128)(2,1)S(1)} %bitcast.12), custom_call_target="tpu_custom_call" | custom-call | tf_op jit(solution)/shard_map/holder/pallas_call | solution.py:355
  43.4 0.1 collective-permute-start
  43.5 1.5 %collective-permute-done = bf16[8,128,128]{2,1,0:T(8,128)(2,1)S(1)} collective-permute-done((bf16[8,128,128]{2,1,0:T(8,128)(2,1)S(1)}, bf16[8,128,128]{2,1,0:T(8,128)(2,1)S(1)}, u32[]{:S(2)}, u32[]{:S(2)}) %collective-permute-start) | collective-permute-done | bytes 262176 | tf_op jit(solution)/shard_map/ppermute | solution.py:392
  45.0 0.1 add_convert_fusion
  45.1 13.2 %all_to_all.10 = bf16[8,128,128]{2,1,0:T(8,128)(2,1)S(1)} all-to-all(bf16[8,128,128]{2,1,0:T(8,128)(2,1)S(1)} %add_convert_fusion), channel_id=1, replica_groups={{0,2,4,6,8,10,12,14},{1,3,5,7,9,11,13,15},{16,18,20,22,24,26,28,30},{17..., dimensions={0} | all-to-all | bytes 524288 | tf_op jit(solution)/shard_map/all_to_all | solution.py:395
  58.3 0.0 copy-done.1
  58.3 0.6 %reshape.15 = bf16[2,1,8192]{2,0,1:T(2,128)(2,1)} reshape(bf16[128,128]{1,0:T(8,128)(2,1)S(1)} %add_convert_fusion.1) | data formatting | bytes 65536 | tf_op jit(solution)/shard_map/reshape | solution.py:397
  (2 shorter events, 0.1 us)
Async XLA Ops:
  16.5 18.0 %all-to-all-start = ((bf16[16,72,128]{2,1,0:T(8,128)(2,1)}), bf16[16,72,128]{2,1,0:T(8,128)(2,1)S(1)}, u32[]{:S(2)}, u32[]{:S(2)}) async-start(bf16[16,72,128]{2,1,0:T(8,128)(2,1)} %get-tuple-element.13), calls=%async_computation | async-start | bytes 589824 | tf_op jit(solution)/shard_map/all_to_all | solution.py:389
  23.9 34.4 %copy-start.1 = (f32[128,128]{1,0:T(8,128)S(1)}, f32[128,128]{1,0:T(8,128)}, u32[]{:S(2)}) copy-start(f32[128,128]{1,0:T(8,128)} %get-tuple-element.11) | copy-start | bytes 196612
  34.5 3.4 %copy-start = (bf16[512,8,8,128]{3,2,1,0:T(8,128)(2,1)S(1)}, bf16[512,8,8,128]{3,2,1,0:T(8,128)(2,1)}, u32[]{:S(2)}) copy-start(bf16[512,8,8,128]{3,2,1,0:T(8,128)(2,1)} %copy.13) | copy-start | bytes 25165828
  43.4 1.6 %collective-permute-start = (bf16[8,128,128]{2,1,0:T(8,128)(2,1)S(1)}, bf16[8,128,128]{2,1,0:T(8,128)(2,1)S(1)}, u32[]{:S(2)}, u32[]{:S(2)}) collective-permute-start(bf16[8,128,128]{2,1,0:T(8,128)(2,1)S(1)} %get-tuple-element.16), channel_id=1, source_target_pairs={{0,1},{1,0},{2,3},{3,2},{4,5},{5,4},{6,7},{7,6},{8,9},{9,8},{10,11... | collective-permute-start | bytes 786440 | tf_op jit(solution)/shard_map/ppermute | solution.py:392

commit v3 on v2

--- a/solution.py
+++ b/solution.py
@@ -65,45 +65,56 @@
     scale = HEAD_SIZE ** -0.5
     length = len_ref[0]
 
-    moves = []
-    for i, (src, dst) in enumerate((
-        (kl_hbm, kl_ref), (rk_hbm, rk_ref), (q_hbm, q_ref), (nk_hbm, nk_ref), (iv_hbm, iv_ref), (sm_hbm, sm_ref),
-        (ch_hbm, ch_ref), (base_hbm, base_ref), (off_hbm, off_ref), (tab_hbm, tab_ref),
-    )):
-        move = pltpu.make_async_copy(src, dst, sems.at[i])
+    half = 4 * LANES
+    count = [0]
+
+    def bring(src, dst):
+        move = pltpu.make_async_copy(src, dst, sems.at[count[0]])
         move.start()
-        moves.append(move)
+        count[0] += 1
+        return move
+
+    lefts = []
+    for t in range(chunks):
+        at = slice(t * 2 * half, (t + 1) * 2 * half)
+        lefts.append(bring(kl_hbm.at[:, at], kl_ref.at[:, at]))
+    right = bring(rk_hbm, rk_ref)
+    small = [bring(*x) for x in (
+        (q_hbm, q_ref), (nk_hbm, nk_ref), (iv_hbm, iv_ref), (sm_hbm, sm_ref), (ch_hbm, ch_ref),
+        (base_hbm, base_ref), (off_hbm, off_ref),
+    )]
+    per_chunk = BLOCK_TOKENS // 2
+    tables = []
+    for t in range(chunks):
+        at = slice(t * per_chunk, (t + 1) * per_chunk)
+        tables.append(bring(tab_hbm.at[at], tab_ref.at[at]))
 
     lane = lax.broadcasted_iota(jnp.int32, (1, HEAD_SIZE), 1)
     low = lane < HALF
-    half = 4 * LANES
     to = lax.broadcasted_iota(jnp.int32, (1, half), 1)
     pm[...] = jnp.where(
         lax.broadcasted_iota(jnp.int32, (half, half), 0) == (to % HALF) * BLOCK_TOKENS + to // HALF, 1.0, 0.0
     ).astype(BF16)
 
-    for move in moves[:2]:
-        move.wait()
-
-    def order(i, _):
-        at = pl.multiple_of(i * 2 * half, 2 * half)
-        a = mm(kl_ref[:, pl.ds(at, half)], pm[...])
-        b = mm(kl_ref[:, pl.ds(at + half, half)], pm[...])
+    for i in range(chunks):
+        lefts[i].wait()
+        at = i * 2 * half
+        a = mm(kl_ref[:, at:at + half], pm[...])
+        b = mm(kl_ref[:, at + half:at + 2 * half], pm[...])
         for m in range(BLOCK_TOKENS // 2):
             x = a[:, m * LANES:(m + 1) * LANES]
             y = b[:, m * LANES:(m + 1) * LANES]
             even = jnp.where(low, x, pltpu.roll(y, HALF, 1))
             odd = jnp.where(low, pltpu.roll(x, HALF, 1), y)
-            lp[i * (BLOCK_TOKENS // 2) + m] = jnp.concatenate([even, odd], axis=1).astype(BF16)
-        return _
-
-    lax.fori_loop(0, chunks, order, 0)
+            lp[i * per_chunk + m] = jnp.concatenate([even, odd], axis=1).astype(BF16)
+
+    right.wait()
     for h in range(heads):
         rt[h * HEAD_SIZE:(h + 1) * HEAD_SIZE, :] = (
             rk_ref[:, h * HEAD_SIZE:(h + 1) * HEAD_SIZE].astype(F32).T.astype(BF16)
         )
 
-    for move in moves[2:9]:
+    for move in small:
         move.wait()
     x = q_ref[...].astype(F32)
     for k in range(per_step):
@@ -152,9 +163,7 @@
                 pieces.append(jnp.concatenate([x, z] if hh == 0 else [z, x], axis=1))
         qp[p] = jnp.concatenate(pieces, axis=0).astype(BF16)
 
-    moves[9].wait()
-
-    def keys(i, _):
+    def keys(i):
         ct = tab_ref[i, 0]
         st = tab_ref[i, 1]
         raw = mm(rt[...], lp[i])
@@ -164,22 +173,24 @@
             kk[i, h * HEAD_SIZE:(h + 1) * HEAD_SIZE, :] = jnp.concatenate(
                 [a * ct - c * st, c * ct + a * st], axis=0
             ).astype(BF16)
-        return _
-
-    lax.fori_loop(0, lp.shape[0], keys, 0, unroll=4)
-
-    def scores(i, _):
-        at = i // (BLOCK_TOKENS // 2)
-        j = 2 * (i % (BLOCK_TOKENS // 2))
+
+    for t in range(chunks):
+        tables[t].wait()
+        for i in range(t * per_chunk, (t + 1) * per_chunk):
+            keys(i)
+
+    def scores(i):
+        at = i // per_chunk
+        j = 2 * (i % per_chunk)
         for p in range(pairs):
             out = mm(qp[p], kk[i, 2 * p * HEAD_SIZE:2 * (p + 1) * HEAD_SIZE, :]) * scale
             for s in range(steps):
                 to_rows = slice(s * per_step + 2 * p * group, s * per_step + 2 * (p + 1) * group)
                 for jj in range(2):
                     sc[at, j + jj, to_rows, :] = out[s * 2 * group:(s + 1) * 2 * group, jj * LANES:(jj + 1) * LANES]
-        return _
-
-    lax.fori_loop(0, lp.shape[0], scores, 0, unroll=4)
+
+    for i in range(lp.shape[0]):
+        scores(i)
 
     wide = steps * n_sel
     entry = lax.broadcasted_iota(jnp.int32, (1, wide), 1)
@@ -192,33 +203,36 @@
     sub = lax.broadcasted_iota(jnp.int32, (16, blocks), 0)
     sub_e = lax.broadcasted_iota(jnp.int32, (8, wide), 0)
 
-    def weigh(h, _):
-        picked = jnp.concatenate([ch_ref[pl.ds(s * heads + h, 1), :] for s in range(steps)], axis=1)
+    def weigh(h):
+        picked = jnp.concatenate([ch_ref[s * heads + h:s * heads + h + 1, :] for s in range(steps)], axis=1)
         hot = jnp.where(block_i == picked, 1.0, 0.0).astype(BF16)
-        row = sm_ref[pl.ds(h, 1), :]
+        row = sm_ref[h:h + 1, :]
         kb = row // pool
         inside = row - kb * pool
         hi = inside // 256
         lo = inside - hi * 256
         extra = jnp.where(sub == 0, hi, jnp.where(sub == 1, lo, jnp.where(sub == 2, kb, 0))).astype(F32).astype(BF16)
-        got = mm(extra, hot)
+        terms = [extra]
+        heres = []
+        for s in range(steps):
+            here = slice((s * heads + h) * group, (s * heads + h + 1) * group)
+            heres.append(here)
+            x = jnp.concatenate(
+                [jnp.concatenate([sc[t, j, here, :] for t in range(chunks)], axis=1) for j in range(BLOCK_TOKENS)],
+                axis=0,
+            )
+            terms += split3(x)
+        got = mm(jnp.concatenate(terms, axis=0), hot)
         kb = got[2:3, :].astype(jnp.int32)
         kh = jnp.where(keeper_i == kb, 1.0, 0.0)
         rank_e = jnp.sum(kh * mm(kh.astype(BF16), before), axis=0, keepdims=True)
         slot = kb * share + rank_e.astype(jnp.int32) + (entry // n_sel) * slots
         pick = jnp.where(slot_i == slot, 1.0, 0.0).astype(BF16)
         xs = None
-        heres = []
+        size = BLOCK_TOKENS * group
         for s in range(steps):
-            here = pl.ds(pl.multiple_of((s * heads + h) * group, group), group)
-            heres.append(here)
-            x = jnp.concatenate(
-                [jnp.concatenate([sc[t, j, here, :] for t in range(chunks)], axis=1) for j in range(BLOCK_TOKENS)],
-                axis=0,
-            )
-            g = mm(jnp.concatenate(split3(x), axis=0), hot)
-            size = BLOCK_TOKENS * group
-            g = (g[:size] + g[size:2 * size]) + g[2 * size:]
+            at = extra.shape[0] + 3 * s * size
+            g = (got[at:at + size] + got[at + size:at + 2 * size]) + got[at + 2 * size:at + 3 * size]
             xs = g if xs is None else jnp.where(entry // n_sel == s, g, xs)
         pos = picked * BLOCK_TOKENS
         xs = [
@@ -249,9 +263,9 @@
         for t in range(planes):
             for s in range(steps):
                 osc[t, heres[s], :] = o[t * group:(t + 1) * group, s * slots:(s + 1) * slots]
-        return _
-
-    lax.fori_loop(0, heads, weigh, 0, unroll=2)
+
+    for h in range(heads):
+        weigh(h)
     fresh_ref[...] = mm(fw_scr[...].astype(BF16), vr[...].astype(BF16))
 
     turned = [osc[t].T for t in range(planes)]
@@ -283,7 +297,7 @@
         in_specs=[pl.BlockSpec(memory_space=pltpu.SMEM)] + [hbm] * len(operands),
         out_specs=(vmem, vmem),
         scratch_shapes=[pltpu.VMEM(x.shape, x.dtype) for x in operands] + [
-            pltpu.SemaphoreType.DMA((len(operands),)),
+            pltpu.SemaphoreType.DMA((len(operands) - 2 + 2 * (blocks // LANES),)),
             pltpu.VMEM((tokens // (2 * LANES), rank, 2 * LANES), BF16),
             pltpu.VMEM((tokens // (2 * LANES), heads * HEAD_SIZE, 2 * LANES), BF16),
             pltpu.VMEM((heads * HEAD_SIZE, rank), BF16),
@@ -306,11 +320,19 @@
     return w, fresh
 
 
-def holder_kernel(share, combos, par_ref, w_ref, v_ref, keep_ref, send_ref, idx_v, idx_s, isem):
+def holder_kernel(share, combos, par_ref, w_ref, v_hbm, keep_ref, send_ref, v_ref, wide, idx_v, idx_s, vsems, isem):
     n, wire, rows = w_ref.shape
     group = rows // combos
     body = BLOCK_TOKENS * share
     fuse = max(1, min(combos, 256 // body))
+    parts = vsems.shape[0]
+    size = v_ref.shape[0] // parts
+    loads = []
+    for i in range(parts):
+        at = pl.ds(i * size, size)
+        load = pltpu.make_async_copy(v_hbm.at[at], v_ref.at[at], vsems.at[i])
+        load.start()
+        loads.append(load)
     raw = w_ref[:, body:body + share, :].astype(F32).reshape(n * share, rows).astype(BF16)
     ci = lax.broadcasted_iota(jnp.int32, (combos, rows), 0)
     li = lax.broadcasted_iota(jnp.int32, (combos, rows), 1)
@@ -326,19 +348,27 @@
     ).astype(BF16)
     rc = lax.broadcasted_iota(jnp.int32, (rows, width), 0) // group
     own = (rc % fuse) == lax.broadcasted_iota(jnp.int32, (rows, width), 1) // body
+
+    def spread(r, _):
+        wt = w_ref[r, :body, :].astype(F32).T.astype(BF16)
+        wide[r] = jnp.where(own, mm(wt, turn), 0.0).astype(BF16)
+        return _
+
+    lax.fori_loop(0, n, spread, 0, unroll=4)
     fetch.wait()
+    for load in loads:
+        load.wait()
     par = par_ref[0]
 
     def one(r):
-        wt = w_ref[r, :body, :].astype(F32).T.astype(BF16)
-        wide = jnp.where(own, mm(wt, turn), 0.0).astype(BF16)
         outs = []
         for g in range(combos // fuse):
             tiles = []
             for c in range(fuse):
                 for i in range(share):
                     tiles.append(v_ref[idx_s[g * fuse + c, r * share + i]])
-            outs.append(mm(wide[g * fuse * group:(g + 1) * fuse * group, :], jnp.concatenate(tiles, axis=0)))
+            at = slice(g * fuse * group, (g + 1) * fuse * group)
+            outs.append(mm(wide[r, at, :], jnp.concatenate(tiles, axis=0)))
         return jnp.concatenate(outs, axis=0)
 
     def step(m, _):
@@ -346,26 +376,31 @@
         keep_ref[m] = one(2 * m + par)
         return _
 
-    lax.fori_loop(0, n // 2, step, 0)
+    lax.fori_loop(0, n // 2, step, 0, unroll=2)
 
 
 def holder(par, w, v, share, combos):
     n, wire, rows = w.shape
     vmem = pl.BlockSpec(memory_space=pltpu.VMEM)
+    body = BLOCK_TOKENS * share
+    fuse = max(1, min(combos, 256 // body))
     return pl.pallas_call(
         functools.partial(holder_kernel, share, combos),
         out_shape=(
             jax.ShapeDtypeStruct((n // 2, rows, HEAD_SIZE), F32),
             jax.ShapeDtypeStruct((n // 2, rows, HEAD_SIZE), BF16),
         ),
-        in_specs=[pl.BlockSpec(memory_space=pltpu.SMEM), vmem, vmem],
+        in_specs=[pl.BlockSpec(memory_space=pltpu.SMEM), vmem, pl.BlockSpec(memory_space=pl.ANY)],
         out_specs=(vmem, vmem),
         scratch_shapes=[
+            pltpu.VMEM(v.shape, v.dtype),
+            pltpu.VMEM((n, rows, fuse * body), BF16),
             pltpu.VMEM((combos, n * share), jnp.int32),
             pltpu.SMEM((combos, n * share), jnp.int32),
+            pltpu.SemaphoreType.DMA((4,)),
             pltpu.SemaphoreType.DMA,
         ],
-        compiler_params=pltpu.CompilerParams(vmem_limit_bytes=20 * 1024 * 1024),
+        compiler_params=pltpu.CompilerParams(vmem_limit_bytes=52 * 1024 * 1024),
         name="holder",
     )(par, w, v)
 

time: 59.3 us -> 55.1 us (0.929)
  local copies, waits for them, and re-layouts: 12.8 us -> 9.4 us
  Pallas kernels: 21.4 us -> 20.7 us
    unnamed x5 -> x3, local copies, waits for them, and re-layouts: 12.2 us -> 8.77 us
    pallas_call x1, Pallas kernels: 15.9 us -> 13.9 us  [owner(): pl.pallas_call(functools.partial(owner_kernel, share, pool, n), out_shape...]
    pallas_call x1, Pallas kernels: 5.56 us -> 6.85 us  [holder(): pl.pallas_call(functools.partial(holder_kernel, share, combos), out_shape...]
  transfers between devices with their start and end apart: 2 -> 2, of which waited for: 2 -> 2; matrix products, arithmetic and copies ran while one was open for 15% -> 16% of each run, Pallas kernels for 0% -> 0%
where the time goes in v3:
time: 55.1 us; the launch traced here: 54.8 us
  Pallas kernels  20.7 us (38%)
  blocking collectives  13.2 us (24%)
  local copies, waits for them, and re-layouts  9.4 us (17%)
  starting transfers between devices  7.44 us (14%)
  waiting for transfers between devices  3.31 us (6%)
  between operations  0.71 us (1%)
    pallas_call x1, Pallas kernels, owner(): pl.pallas_call(functools.partial(owner_kernel, share, pool, n), out_shape...  13.9 us
    all_to_all x1, blocking collectives, per_device(): lax.all_to_all(both, 'store', split_axis=0, concat_axis=0, tiled=True, ax...  13.2 us
    unnamed x3, local copies, waits for them, and re-layouts  8.77 us
    all_to_all x1, starting transfers between devices, per_device(): w = lax.all_to_all(w, 'store', split_axis=0, concat_axis=0, tiled=True)  7.37 us
    pallas_call x1, Pallas kernels, holder(): pl.pallas_call(functools.partial(holder_kernel, share, combos), out_shape...  6.85 us
    all_to_all x1, waiting for transfers between devices, per_device(): w = lax.all_to_all(w, 'store', split_axis=0, concat_axis=0, tiled=True)  1.79 us
    ppermute x1, waiting for transfers between devices, per_device(): other = lax.ppermute(send, 'store', [(i, i ^ 1) for i in range(n)])  1.52 us
  transfers between devices with their start and end apart: 2, of which 2 were waited for; matrix products, arithmetic and copies ran while one was open for 16% of the time, Pallas kernels for 0%

profile of v3, /device:TPU:0, one launch (start us, length us, event | category | flops | bytes accessed | tf_op | source)
XLA Modules:
  0.0 54.8 jit_solution(13749663402280517368)
XLA Ops:
  0.7 13.9 %owner.1 = (bf16[16,72,128]{2,1,0:T(8,128)(2,1)}, f32[128,128]{1,0:T(8,128)}) custom-call(s32[1]{0:T(128)S(6)} %copy.14.len_ref, bf16[2,8192]{1,0:T(2,128)(2,1)} %bitcast.16, bf16[2,1024]{1,0:T(2,128)(2,1)} %bitcast.19, bf16[2,1024]{1,0:T(2,128)(2,1)} %bitcast.20, bf16[160,4096]{1,0:T(8,128)(2,1)} %bitcast.14, bf16[160,1024]{1,0:T(8,128)(2,1)} %bitcast.15, ...), custom_call_target="tpu_custom_call" | custom-call | tf_op jit(solution)/shard_map/owner/pallas_call | solution.py:294
  14.5 7.4 %all-to-all-start = ((bf16[16,72,128]{2,1,0:T(8,128)(2,1)}), bf16[16,72,128]{2,1,0:T(8,128)(2,1)S(1)}, u32[]{:S(2)}, u32[]{:S(2)}) async-start(bf16[16,72,128]{2,1,0:T(8,128)(2,1)} %get-tuple-element.13), calls=%async_computation | async-start | bytes 589824 | tf_op jit(solution)/shard_map/all_to_all | solution.py:424
  21.9 8.8 %copy.13 = bf16[512,8,8,128]{3,2,1,0:T(8,128)(2,1)} copy(bf16[512,8,8,128]{3,1,2,0:T(8,128)(2,1)} %bitcast.13) | data formatting | bytes 16777216
  30.7 0.0 copy-start
  30.7 1.8 %all-to-all-done.w_ref = bf16[16,72,128]{2,1,0:T(8,128)(2,1)S(1)} async-done(((bf16[16,72,128]{2,1,0:T(8,128)(2,1)}), bf16[16,72,128]{2,1,0:T(8,128)(2,1)S(1)}, u32[]{:S(2)}, u32[]{:S(2)}) %all-to-all-start) | async-done | bytes 294944 | tf_op jit(solution)/shard_map/all_to_all | solution.py:424
  32.5 6.9 %holder.1 = (f32[8,128,128]{2,1,0:T(8,128)S(1)}, bf16[8,128,128]{2,1,0:T(8,128)(2,1)S(1)}) custom-call(s32[1]{0:T(128)} %bitcast.8.par_ref, bf16[16,72,128]{2,1,0:T(8,128)(2,1)S(1)} %all-to-all-done.w_ref, bf16[4096,8,128]{2,1,0:T(8,128)(2,1)} %bitcast.12), custom_call_target="tpu_custom_call" | custom-call | tf_op jit(solution)/shard_map/holder/pallas_call | solution.py:387
  39.3 0.1 collective-permute-start
  39.4 1.5 %collective-permute-done = bf16[8,128,128]{2,1,0:T(8,128)(2,1)S(1)} collective-permute-done((bf16[8,128,128]{2,1,0:T(8,128)(2,1)S(1)}, bf16[8,128,128]{2,1,0:T(8,128)(2,1)S(1)}, u32[]{:S(2)}, u32[]{:S(2)}) %collective-permute-start) | collective-permute-done | bytes 262176 | tf_op jit(solution)/shard_map/ppermute | solution.py:427
  40.9 0.1 add_convert_fusion
  41.0 13.2 %all_to_all.10 = bf16[8,128,128]{2,1,0:T(8,128)(2,1)S(1)} all-to-all(bf16[8,128,128]{2,1,0:T(8,128)(2,1)S(1)} %add_convert_fusion), channel_id=1, replica_groups={{0,2,4,6,8,10,12,14},{1,3,5,7,9,11,13,15},{16,18,20,22,24,26,28,30},{17..., dimensions={0} | all-to-all | bytes 524288 | tf_op jit(solution)/shard_map/all_to_all | solution.py:430
  54.2 0.0 copy-done
  54.2 0.6 %reshape.15 = bf16[2,1,8192]{2,0,1:T(2,128)(2,1)} reshape(bf16[128,128]{1,0:T(8,128)(2,1)S(1)} %add_convert_fusion.1) | data formatting | bytes 65536 | tf_op jit(solution)/shard_map/reshape | solution.py:432
  (2 shorter events, 0.0 us)
Async XLA Ops:
  14.5 18.0 %all-to-all-start = ((bf16[16,72,128]{2,1,0:T(8,128)(2,1)}), bf16[16,72,128]{2,1,0:T(8,128)(2,1)S(1)}, u32[]{:S(2)}, u32[]{:S(2)}) async-start(bf16[16,72,128]{2,1,0:T(8,128)(2,1)} %get-tuple-element.13), calls=%async_computation | async-start | bytes 589824 | tf_op jit(solution)/shard_map/all_to_all | solution.py:424
  30.7 23.5 %copy-start = (f32[128,128]{1,0:T(8,128)S(1)}, f32[128,128]{1,0:T(8,128)}, u32[]{:S(2)}) copy-start(f32[128,128]{1,0:T(8,128)} %get-tuple-element.11) | copy-start | bytes 196612
  39.3 1.6 %collective-permute-start = (bf16[8,128,128]{2,1,0:T(8,128)(2,1)S(1)}, bf16[8,128,128]{2,1,0:T(8,128)(2,1)S(1)}, u32[]{:S(2)}, u32[]{:S(2)}) collective-permute-start(bf16[8,128,128]{2,1,0:T(8,128)(2,1)S(1)} %get-tuple-element.16), channel_id=1, source_target_pairs={{0,1},{1,0},{2,3},{3,2},{4,5},{5,4},{6,7},{7,6},{8,9},{9,8},{10,11... | collective-permute-start | bytes 786440 | tf_op jit(solution)/shard_map/ppermute | solution.py:427

commit v4 on v3

--- a/solution.py
+++ b/solution.py
@@ -49,7 +49,7 @@
     share, pool, keepers, len_ref, q_hbm, nk_hbm, iv_hbm, kl_hbm, rk_hbm, sm_hbm, ch_hbm, tab_hbm, base_hbm, off_hbm,
     w_ref, fresh_ref,
     q_ref, nk_ref, iv_ref, kl_ref, rk_ref, sm_ref, ch_ref, tab_ref, base_ref, off_ref, sems,
-    lp, kk, rt, qp, qr, nr, vr, sc, fs_scr, fm_scr, fw_scr, pm, osc,
+    lp, kk, rt, qp, qr, nr, vr, sc, fs_scr, fm_scr, fw_scr, pm, got_scr, lhs_scr, osc,
 ):
     rank, tokens = kl_ref.shape
     heads, blocks = sm_ref.shape
@@ -196,16 +196,23 @@
     entry = lax.broadcasted_iota(jnp.int32, (1, wide), 1)
     block_i = lax.broadcasted_iota(jnp.int32, (blocks, wide), 0)
     keeper_i = lax.broadcasted_iota(jnp.int32, (keepers, wide), 0)
-    slot_i = lax.broadcasted_iota(jnp.int32, (steps * slots, wide), 0)
+    slot_i = lax.broadcasted_iota(jnp.int32, (wide, steps * slots), 1).astype(F32)
     e0 = lax.broadcasted_iota(jnp.int32, (wide, wide), 0)
     e1 = lax.broadcasted_iota(jnp.int32, (wide, wide), 1)
     before = jnp.where(jnp.logical_and(e0 // n_sel == e1 // n_sel, e0 < e1), 1.0, 0.0).astype(BF16)
     sub = lax.broadcasted_iota(jnp.int32, (16, blocks), 0)
     sub_e = lax.broadcasted_iota(jnp.int32, (8, wide), 0)
 
-    def weigh(h):
-        picked = jnp.concatenate([ch_ref[s * heads + h:s * heads + h + 1, :] for s in range(steps)], axis=1)
-        hot = jnp.where(block_i == picked, 1.0, 0.0).astype(BF16)
+    size = BLOCK_TOKENS * group
+    heres = [
+        [slice((s * heads + h) * group, (s * heads + h + 1) * group) for s in range(steps)] for h in range(heads)
+    ]
+    chosen = [
+        jnp.concatenate([ch_ref[s * heads + h:s * heads + h + 1, :] for s in range(steps)], axis=1)
+        for h in range(heads)
+    ]
+    for h in range(heads):
+        hot = jnp.where(block_i == chosen[h], 1.0, 0.0).astype(BF16)
         row = sm_ref[h:h + 1, :]
         kb = row // pool
         inside = row - kb * pool
@@ -213,28 +220,36 @@
         lo = inside - hi * 256
         extra = jnp.where(sub == 0, hi, jnp.where(sub == 1, lo, jnp.where(sub == 2, kb, 0))).astype(F32).astype(BF16)
         terms = [extra]
-        heres = []
         for s in range(steps):
-            here = slice((s * heads + h) * group, (s * heads + h + 1) * group)
-            heres.append(here)
             x = jnp.concatenate(
-                [jnp.concatenate([sc[t, j, here, :] for t in range(chunks)], axis=1) for j in range(BLOCK_TOKENS)],
+                [
+                    jnp.concatenate([sc[t, j, heres[h][s], :] for t in range(chunks)], axis=1)
+                    for j in range(BLOCK_TOKENS)
+                ],
                 axis=0,
             )
             terms += split3(x)
-        got = mm(jnp.concatenate(terms, axis=0), hot)
-        kb = got[2:3, :].astype(jnp.int32)
-        kh = jnp.where(keeper_i == kb, 1.0, 0.0)
-        rank_e = jnp.sum(kh * mm(kh.astype(BF16), before), axis=0, keepdims=True)
-        slot = kb * share + rank_e.astype(jnp.int32) + (entry // n_sel) * slots
-        pick = jnp.where(slot_i == slot, 1.0, 0.0).astype(BF16)
+        got_scr[h] = mm(jnp.concatenate(terms, axis=0), hot)
+
+    kbs = [got_scr[h, 2:3, :] for h in range(heads)]
+    khs = jnp.concatenate([jnp.where(keeper_i == kb.astype(jnp.int32), 1.0, 0.0) for kb in kbs], axis=0)
+    ranks = khs * mm(khs.astype(BF16), before)
+    first = ((entry // n_sel) * slots).astype(F32)
+    slot = jnp.concatenate(
+        [
+            kbs[h] * share + first + jnp.sum(ranks[h * keepers:(h + 1) * keepers], axis=0, keepdims=True)
+            for h in range(heads)
+        ],
+        axis=0,
+    ).T
+
+    for h in range(heads):
         xs = None
-        size = BLOCK_TOKENS * group
         for s in range(steps):
-            at = extra.shape[0] + 3 * s * size
-            g = (got[at:at + size] + got[at + size:at + 2 * size]) + got[at + 2 * size:at + 3 * size]
+            at = 16 + 3 * s * size
+            g = (got_scr[h, at:at + size] + got_scr[h, at + size:at + 2 * size]) + got_scr[h, at + 2 * size:at + 3 * size]
             xs = g if xs is None else jnp.where(entry // n_sel == s, g, xs)
-        pos = picked * BLOCK_TOKENS
+        pos = chosen[h] * BLOCK_TOKENS
         xs = [
             jnp.where(pos + j < length, xs[j * group:(j + 1) * group, :], -jnp.inf) for j in range(BLOCK_TOKENS)
         ]
@@ -244,7 +259,7 @@
         for s in range(steps):
             mine = entry // n_sel == s
             t = jnp.max(jnp.where(mine, most, -jnp.inf), axis=1, keepdims=True)
-            t = jnp.maximum(t, fm_scr[heres[s], :])
+            t = jnp.maximum(t, fm_scr[heres[h][s], :])
             tops.append(t)
             top = jnp.broadcast_to(t, most.shape) if top is None else jnp.where(mine, t, top)
         es = [jnp.exp(x - top) for x in xs]
@@ -252,20 +267,21 @@
         inv = None
         for s in range(steps):
             mine = entry // n_sel == s
-            fe = jnp.exp(fs_scr[heres[s], :] - tops[s])
+            fe = jnp.exp(fs_scr[heres[h][s], :] - tops[s])
             total = jnp.sum(jnp.where(mine, added, 0.0), axis=1, keepdims=True)
             one = 1.0 / (total + jnp.sum(fe, axis=1, keepdims=True))
-            fw_scr[heres[s], :] = fe * one
+            fw_scr[heres[h][s], :] = fe * one
             inv = jnp.broadcast_to(one, most.shape) if inv is None else jnp.where(mine, one, inv)
-        tail = jnp.where(sub_e < 2, got[:8, :], 0.0)
-        lhs = jnp.concatenate([e * inv for e in es] + [tail, jnp.zeros_like(tail)], axis=0).astype(BF16)
-        o = mm(lhs, pick, NT)
+        tail = jnp.where(sub_e < 2, got_scr[h, :8, :], 0.0)
+        lhs_scr[h] = jnp.concatenate([e * inv for e in es] + [tail, jnp.zeros_like(tail)], axis=0).astype(BF16)
+
+    for h in range(heads):
+        pick = jnp.where(slot_i == slot[:, h:h + 1], 1.0, 0.0).astype(BF16)
+        o = mm(lhs_scr[h], pick)
         for t in range(planes):
             for s in range(steps):
-                osc[t, heres[s], :] = o[t * group:(t + 1) * group, s * slots:(s + 1) * slots]
-
-    for h in range(heads):
-        weigh(h)
+                osc[t, heres[h][s], :] = o[t * group:(t + 1) * group, s * slots:(s + 1) * slots]
+
     fresh_ref[...] = mm(fw_scr[...].astype(BF16), vr[...].astype(BF16))
 
     turned = [osc[t].T for t in range(planes)]
@@ -310,6 +326,8 @@
             pltpu.VMEM((rows, 1), F32),
             pltpu.VMEM((rows, fresh_rows), F32),
             pltpu.VMEM((4 * LANES, 4 * LANES), BF16),
+            pltpu.VMEM((heads, 16 + 3 * rows // heads * BLOCK_TOKENS, combos // heads * n_sel), F32),
+            pltpu.VMEM((heads, (planes + 1) * rows // combos, combos // heads * n_sel), BF16),
             pltpu.VMEM((planes, rows, slots), F32),
         ],
         compiler_params=pltpu.CompilerParams(vmem_limit_bytes=60 * 1024 * 1024),
@@ -318,6 +336,71 @@
     if not direct:
         w = w.reshape(planes, n, share, rows).transpose(1, 0, 2, 3).reshape(n, planes * share, rows)
     return w, fresh
+
+
+def tile_kernel(v_hbm, out_hbm, buf, out, sems, out_sems):
+    pool, width = buf.shape
+    chunks = width // LANES
+    parts = sems.shape[0]
+    size = pool // parts
+    run = 32
+    loads = []
+    for i in range(parts):
+        at = pl.ds(i * size, size)
+        load = pltpu.make_async_copy(v_hbm.at[at, :], buf.at[at, :], sems.at[i])
+        load.start()
+        loads.append(load)
+    n = run * chunks
+    to = lax.broadcasted_iota(jnp.int32, (n, n), 0)
+    turn = jnp.where(
+        lax.broadcasted_iota(jnp.int32, (n, n), 1) == (to % chunks) * run + to // chunks, 1.0, 0.0
+    ).astype(BF16)
+
+    def one(k, _):
+        at = pl.multiple_of(k * 2 * run, 2 * run)
+        x = jnp.concatenate([
+            jnp.concatenate(
+                [buf[pl.ds(at + g * run, run), c * LANES:(c + 1) * LANES] for c in range(chunks)], axis=0
+            ) for g in range(2)
+        ], axis=1)
+        y = mm(turn, x)
+        for g in range(2):
+            out[pl.ds(at + g * run, run), :, :] = (
+                y[:, g * LANES:(g + 1) * LANES].reshape(run, chunks, LANES).astype(BF16)
+            )
+        return _
+
+    per = size // (2 * run)
+    stores = []
+    for i in range(parts):
+        loads[i].wait()
+        lax.fori_loop(i * per, (i + 1) * per, one, 0, unroll=16)
+        at = pl.ds(i * size, size)
+        store = pltpu.make_async_copy(out.at[at], out_hbm.at[at], out_sems.at[i])
+        store.start()
+        stores.append(store)
+    for store in stores:
+        store.wait()
+
+
+def tile_rows(v):
+    pool, width = v.shape
+    shape = (pool, width // LANES, LANES)
+    return pl.pallas_call(
+        tile_kernel,
+        out_shape=jax.ShapeDtypeStruct(shape, v.dtype),
+        in_specs=[pl.BlockSpec(memory_space=pl.ANY)],
+        out_specs=pl.BlockSpec(memory_space=pl.ANY),
+        scratch_shapes=[
+            pltpu.VMEM(v.shape, v.dtype),
+            pltpu.VMEM(shape, v.dtype),
+            pltpu.SemaphoreType.DMA((4,)),
+            pltpu.SemaphoreType.DMA((4,)),
+        ],
+        compiler_params=pltpu.CompilerParams(vmem_limit_bytes=54 * 1024 * 1024),
+        cost_estimate=pl.CostEstimate(flops=2 * pool * width * 256, bytes_accessed=4 * pool * width, transcendentals=0),
+        name="tile_rows",
+    )(v)
 
 
 def holder_kernel(share, combos, par_ref, w_ref, v_hbm, keep_ref, send_ref, v_ref, wide, idx_v, idx_s, vsems, isem):
@@ -420,7 +503,7 @@
         right_key_factor[0], slot_map[0], chosen.reshape(combos, n_sel), share, n, pool,
     )
     w, store = lax.optimization_barrier((w, value_tile_store))
-    tiles = store.reshape(pool, BLOCK_TOKENS, HEAD_SIZE)
+    tiles = tile_rows(store)
     w = lax.all_to_all(w, "store", split_axis=0, concat_axis=0, tiled=True)
     par = (me % 2).astype(jnp.int32).reshape(1)
     keep, send = holder(par, w, tiles, share, combos)

time: 55.1 us -> 50.7 us (0.920)
  local copies, waits for them, and re-layouts: 9.4 us -> 0.63 us
  waiting for transfers between devices: 3.31 us -> 6.16 us
  Pallas kernels: 20.7 us -> 23.3 us
  blocking collectives: 13.2 us -> 12.1 us
    unnamed x3 -> x2, local copies, waits for them, and re-layouts: 8.77 us -> 0.01 us
    pallas_call x0 -> x1, Pallas kernels: none -> 5.91 us  [tile_rows(): pl.pallas_call(tile_kernel, out_shape=jax.ShapeDtypeStruct(shape, v.dtype...]
    pallas_call x1, Pallas kernels: 13.9 us -> 10.5 us  [owner(): pl.pallas_call(functools.partial(owner_kernel, share, pool, n), out_shape...]
    all_to_all x1, waiting for transfers between devices: 1.79 us -> 4.63 us  [per_device(): w = lax.all_to_all(w, 'store', split_axis=0, concat_axis=0, tiled=True)]
    all_to_all x1, blocking collectives: 13.2 us -> 12.1 us  [per_device(): lax.all_to_all(both, 'store', split_axis=0, concat_axis=0, tiled=True, ax...]
  transfers between devices with their start and end apart: 2 -> 2, of which waited for: 2 -> 2; matrix products, arithmetic and copies ran while one was open for 16% -> 0% of each run, Pallas kernels for 0% -> 12%
where the time goes in v4:
time: 50.7 us; the launch traced here: 50.5 us
  Pallas kernels  23.3 us (46%)
  blocking collectives  12.1 us (24%)
  starting transfers between devices  7.43 us (15%)
  waiting for transfers between devices  6.16 us (12%)
  between operations  0.73 us (1%)
  local copies, waits for them, and re-layouts  0.63 us (1%)
    all_to_all x1, blocking collectives, per_device(): lax.all_to_all(both, 'store', split_axis=0, concat_axis=0, tiled=True, ax...  12.1 us
    pallas_call x1, Pallas kernels, owner(): pl.pallas_call(functools.partial(owner_kernel, share, pool, n), out_shape...  10.5 us
    all_to_all x1, starting transfers between devices, per_device(): w = lax.all_to_all(w, 'store', split_axis=0, concat_axis=0, tiled=True)  7.35 us
    pallas_call x1, Pallas kernels, holder(): pl.pallas_call(functools.partial(holder_kernel, share, combos), out_shape...  6.85 us
    pallas_call x1, Pallas kernels, tile_rows(): pl.pallas_call(tile_kernel, out_shape=jax.ShapeDtypeStruct(shape, v.dtype...  5.91 us
    all_to_all x1, waiting for transfers between devices, per_device(): w = lax.all_to_all(w, 'store', split_axis=0, concat_axis=0, tiled=True)  4.63 us
    ppermute x1, waiting for transfers between devices, per_device(): other = lax.ppermute(send, 'store', [(i, i ^ 1) for i in range(n)])  1.52 us
  transfers between devices with their start and end apart: 2, of which 2 were waited for; matrix products, arithmetic and copies ran while one was open for 0% of the time, Pallas kernels for 12%

profile of v4, /device:TPU:0, one launch (start us, length us, event | category | flops | bytes accessed | tf_op | source)
XLA Modules:
  0.0 50.5 jit_solution(7297257281972687842)
XLA Ops:
  0.7 10.5 %owner.1 = (bf16[16,72,128]{2,1,0:T(8,128)(2,1)}, f32[128,128]{1,0:T(8,128)}) custom-call(s32[1]{0:T(128)S(6)} %copy.13.len_ref, bf16[2,8192]{1,0:T(2,128)(2,1)} %bitcast.12, bf16[2,1024]{1,0:T(2,128)(2,1)} %bitcast.15, bf16[2,1024]{1,0:T(2,128)(2,1)} %bitcast.16, bf16[160,4096]{1,0:T(8,128)(2,1)} %bitcast.10, bf16[160,1024]{1,0:T(8,128)(2,1)} %bitcast.11, ...), custom_call_target="tpu_custom_call" | custom-call | tf_op jit(solution)/shard_map/owner/pallas_call | solution.py:310
  11.2 7.4 %all-to-all-start = ((bf16[16,72,128]{2,1,0:T(8,128)(2,1)}), bf16[16,72,128]{2,1,0:T(8,128)(2,1)S(1)}, u32[]{:S(2)}, u32[]{:S(2)}) async-start(bf16[16,72,128]{2,1,0:T(8,128)(2,1)} %get-tuple-element.13), calls=%async_computation | async-start | bytes 589824 | tf_op jit(solution)/shard_map/all_to_all | solution.py:507
  18.6 5.9 %tile_rows.1.v_hbm = bf16[4096,8,128]{2,1,0:T(8,128)(2,1)} custom-call(bf16[4096,1024]{1,0:T(8,128)(2,1)} %v_hbm), custom_call_target="tpu_custom_call" | custom-call | flops 2147483648 | bytes 16777216 | tf_op jit(solution)/shard_map/tile_rows/pallas_call | solution.py:389
  24.5 0.0 copy-start
  24.5 4.6 %all-to-all-done.w_ref = bf16[16,72,128]{2,1,0:T(8,128)(2,1)S(1)} async-done(((bf16[16,72,128]{2,1,0:T(8,128)(2,1)}), bf16[16,72,128]{2,1,0:T(8,128)(2,1)S(1)}, u32[]{:S(2)}, u32[]{:S(2)}) %all-to-all-start) | async-done | bytes 294944 | tf_op jit(solution)/shard_map/all_to_all | solution.py:507
  29.1 6.8 %holder.1 = (f32[8,128,128]{2,1,0:T(8,128)S(1)}, bf16[8,128,128]{2,1,0:T(8,128)(2,1)S(1)}) custom-call(s32[1]{0:T(128)} %bitcast.8.par_ref, bf16[16,72,128]{2,1,0:T(8,128)(2,1)S(1)} %all-to-all-done.w_ref, bf16[4096,8,128]{2,1,0:T(8,128)(2,1)} %tile_rows.1.v_hbm), custom_call_target="tpu_custom_call" | custom-call | tf_op jit(solution)/shard_map/holder/pallas_call | solution.py:470
  36.0 0.1 collective-permute-start
  36.1 1.5 %collective-permute-done = bf16[8,128,128]{2,1,0:T(8,128)(2,1)S(1)} collective-permute-done((bf16[8,128,128]{2,1,0:T(8,128)(2,1)S(1)}, bf16[8,128,128]{2,1,0:T(8,128)(2,1)S(1)}, u32[]{:S(2)}, u32[]{:S(2)}) %collective-permute-start) | collective-permute-done | bytes 262176 | tf_op jit(solution)/shard_map/ppermute | solution.py:510
  37.6 0.1 add_convert_fusion
  37.7 12.1 %all_to_all.10 = bf16[8,128,128]{2,1,0:T(8,128)(2,1)S(1)} all-to-all(bf16[8,128,128]{2,1,0:T(8,128)(2,1)S(1)} %add_convert_fusion), channel_id=1, replica_groups={{0,2,4,6,8,10,12,14},{1,3,5,7,9,11,13,15},{16,18,20,22,24,26,28,30},{17..., dimensions={0} | all-to-all | bytes 524288 | tf_op jit(solution)/shard_map/all_to_all | solution.py:513
  49.8 0.0 copy-done
  49.8 0.6 %reshape.11 = bf16[2,1,8192]{2,0,1:T(2,128)(2,1)} reshape(bf16[128,128]{1,0:T(8,128)(2,1)S(1)} %add_convert_fusion.1) | data formatting | bytes 65536 | tf_op jit(solution)/shard_map/reshape | solution.py:515
  (2 shorter events, 0.1 us)
Async XLA Ops:
  11.2 17.9 %all-to-all-start = ((bf16[16,72,128]{2,1,0:T(8,128)(2,1)}), bf16[16,72,128]{2,1,0:T(8,128)(2,1)S(1)}, u32[]{:S(2)}, u32[]{:S(2)}) async-start(bf16[16,72,128]{2,1,0:T(8,128)(2,1)} %get-tuple-element.13), calls=%async_computation | async-start | bytes 589824 | tf_op jit(solution)/shard_map/all_to_all | solution.py:507
  24.5 25.3 %copy-start = (f32[128,128]{1,0:T(8,128)S(1)}, f32[128,128]{1,0:T(8,128)}, u32[]{:S(2)}) copy-start(f32[128,128]{1,0:T(8,128)} %get-tuple-element.11) | copy-start | bytes 196612
  36.0 1.6 %collective-permute-start = (bf16[8,128,128]{2,1,0:T(8,128)(2,1)S(1)}, bf16[8,128,128]{2,1,0:T(8,128)(2,1)S(1)}, u32[]{:S(2)}, u32[]{:S(2)}) collective-permute-start(bf16[8,128,128]{2,1,0:T(8,128)(2,1)S(1)} %get-tuple-element.16), channel_id=1, source_target_pairs={{0,1},{1,0},{2,3},{3,2},{4,5},{5,4},{6,7},{7,6},{8,9},{9,8},{10,11... | collective-permute-start | bytes 786440 | tf_op jit(solution)/shard_map/ppermute | solution.py:510

commit v5 on v4

--- a/solution.py
+++ b/solution.py
@@ -12,6 +12,7 @@
 HALF = HEAD_SIZE // 2
 BLOCK_TOKENS = 8
 LANES = 128
+FAR = 64
 ROPE_BASE = 500000.0
 NT = (((1,), (1,)), ((), ()))
 NN = (((1,), (0,)), ((), ()))
@@ -31,11 +32,9 @@
     angle = (pos[:, None, :] * freq[None, :, None]).astype(np.float64)
     keys = np.stack([np.cos(angle), np.sin(angle)], axis=1).astype(np.float32)
     freq = np.concatenate([freq, freq]).astype(np.float64)
-    rows = np.arange(-(-(blocks + 2) // 8) * 8, dtype=np.float64)[:, None] * BLOCK_TOKENS
-    offs = np.arange(BLOCK_TOKENS, dtype=np.float64)[:, None]
-    base = np.stack([np.cos(rows * freq), np.sin(rows * freq)]).astype(np.float32)
-    off = np.stack([np.cos(offs * freq), np.sin(offs * freq)]).astype(np.float32)
-    return keys, base, off
+    far = np.arange(-(-(blocks * BLOCK_TOKENS // FAR + 2) // 8) * 8, dtype=np.float64) * FAR
+    angle = np.concatenate([far, np.arange(FAR, dtype=np.float64)])[:, None] * freq
+    return keys, np.stack([np.cos(angle), np.sin(angle)]).astype(np.float32)
 
 
 def split3(x):
@@ -46,9 +45,9 @@
 
 
 def owner_kernel(
-    share, pool, keepers, len_ref, q_hbm, nk_hbm, iv_hbm, kl_hbm, rk_hbm, sm_hbm, ch_hbm, tab_hbm, base_hbm, off_hbm,
+    share, pool, keepers, len_ref, q_hbm, nk_hbm, iv_hbm, kl_hbm, rk_hbm, sm_hbm, ch_hbm, tab_hbm, turn_hbm,
     w_ref, fresh_ref,
-    q_ref, nk_ref, iv_ref, kl_ref, rk_ref, sm_ref, ch_ref, tab_ref, base_ref, off_ref, sems,
+    q_ref, nk_ref, iv_ref, kl_ref, rk_ref, sm_ref, ch_ref, tab_ref, turn_ref, sems,
     lp, kk, rt, qp, qr, nr, vr, sc, fs_scr, fm_scr, fw_scr, pm, got_scr, lhs_scr, osc,
 ):
     rank, tokens = kl_ref.shape
@@ -74,20 +73,12 @@
         count[0] += 1
         return move
 
-    lefts = []
-    for t in range(chunks):
-        at = slice(t * 2 * half, (t + 1) * 2 * half)
-        lefts.append(bring(kl_hbm.at[:, at], kl_ref.at[:, at]))
+    small = [bring(*x) for x in ((q_hbm, q_ref), (nk_hbm, nk_ref), (iv_hbm, iv_ref), (turn_hbm, turn_ref))]
     right = bring(rk_hbm, rk_ref)
-    small = [bring(*x) for x in (
-        (q_hbm, q_ref), (nk_hbm, nk_ref), (iv_hbm, iv_ref), (sm_hbm, sm_ref), (ch_hbm, ch_ref),
-        (base_hbm, base_ref), (off_hbm, off_ref),
-    )]
+    left = bring(kl_hbm, kl_ref)
+    table = bring(tab_hbm, tab_ref)
+    maps = [bring(sm_hbm, sm_ref), bring(ch_hbm, ch_ref)]
     per_chunk = BLOCK_TOKENS // 2
-    tables = []
-    for t in range(chunks):
-        at = slice(t * per_chunk, (t + 1) * per_chunk)
-        tables.append(bring(tab_hbm.at[at], tab_ref.at[at]))
 
     lane = lax.broadcasted_iota(jnp.int32, (1, HEAD_SIZE), 1)
     low = lane < HALF
@@ -95,24 +86,6 @@
     pm[...] = jnp.where(
         lax.broadcasted_iota(jnp.int32, (half, half), 0) == (to % HALF) * BLOCK_TOKENS + to // HALF, 1.0, 0.0
     ).astype(BF16)
-
-    for i in range(chunks):
-        lefts[i].wait()
-        at = i * 2 * half
-        a = mm(kl_ref[:, at:at + half], pm[...])
-        b = mm(kl_ref[:, at + half:at + 2 * half], pm[...])
-        for m in range(BLOCK_TOKENS // 2):
-            x = a[:, m * LANES:(m + 1) * LANES]
-            y = b[:, m * LANES:(m + 1) * LANES]
-            even = jnp.where(low, x, pltpu.roll(y, HALF, 1))
-            odd = jnp.where(low, pltpu.roll(x, HALF, 1), y)
-            lp[i * per_chunk + m] = jnp.concatenate([even, odd], axis=1).astype(BF16)
-
-    right.wait()
-    for h in range(heads):
-        rt[h * HEAD_SIZE:(h + 1) * HEAD_SIZE, :] = (
-            rk_ref[:, h * HEAD_SIZE:(h + 1) * HEAD_SIZE].astype(F32).T.astype(BF16)
-        )
 
     for move in small:
         move.wait()
@@ -128,12 +101,12 @@
     sign = jnp.where(low, -1.0, 1.0).astype(F32)
 
     def angle(position):
-        b = position // BLOCK_TOKENS
-        j = position - b * BLOCK_TOKENS
-        cb = base_ref[0, pl.ds(b, 1), :]
-        sb = base_ref[1, pl.ds(b, 1), :]
-        cj = off_ref[0, pl.ds(j, 1), :]
-        sj = off_ref[1, pl.ds(j, 1), :]
+        b = position // FAR
+        j = position - b * FAR + turn_ref.shape[1] - FAR
+        cb = turn_ref[0, pl.ds(b, 1), :]
+        sb = turn_ref[1, pl.ds(b, 1), :]
+        cj = turn_ref[0, pl.ds(j, 1), :]
+        sj = turn_ref[1, pl.ds(j, 1), :]
         return cb * cj - sb * sj, (sb * cj + cb * sj) * sign
 
     fresh_keys = []
@@ -163,6 +136,25 @@
                 pieces.append(jnp.concatenate([x, z] if hh == 0 else [z, x], axis=1))
         qp[p] = jnp.concatenate(pieces, axis=0).astype(BF16)
 
+    right.wait()
+    for h in range(heads):
+        rt[h * HEAD_SIZE:(h + 1) * HEAD_SIZE, :] = (
+            rk_ref[:, h * HEAD_SIZE:(h + 1) * HEAD_SIZE].astype(F32).T.astype(BF16)
+        )
+
+    left.wait()
+
+    for i in range(chunks):
+        at = i * 2 * half
+        a = mm(kl_ref[:, at:at + half], pm[...])
+        b = mm(kl_ref[:, at + half:at + 2 * half], pm[...])
+        for m in range(BLOCK_TOKENS // 2):
+            x = a[:, m * LANES:(m + 1) * LANES]
+            y = b[:, m * LANES:(m + 1) * LANES]
+            even = jnp.where(low, x, pltpu.roll(y, HALF, 1))
+            odd = jnp.where(low, pltpu.roll(x, HALF, 1), y)
+            lp[i * per_chunk + m] = jnp.concatenate([even, odd], axis=1).astype(BF16)
+
     def keys(i):
         ct = tab_ref[i, 0]
         st = tab_ref[i, 1]
@@ -174,11 +166,6 @@
                 [a * ct - c * st, c * ct + a * st], axis=0
             ).astype(BF16)
 
-    for t in range(chunks):
-        tables[t].wait()
-        for i in range(t * per_chunk, (t + 1) * per_chunk):
-            keys(i)
-
     def scores(i):
         at = i // per_chunk
         j = 2 * (i % per_chunk)
@@ -189,9 +176,15 @@
                 for jj in range(2):
                     sc[at, j + jj, to_rows, :] = out[s * 2 * group:(s + 1) * 2 * group, jj * LANES:(jj + 1) * LANES]
 
+    table.wait()
     for i in range(lp.shape[0]):
-        scores(i)
-
+        keys(i)
+        if i > 0:
+            scores(i - 1)
+    scores(lp.shape[0] - 1)
+
+    for move in maps:
+        move.wait()
     wide = steps * n_sel
     entry = lax.broadcasted_iota(jnp.int32, (1, wide), 1)
     block_i = lax.broadcasted_iota(jnp.int32, (blocks, wide), 0)
@@ -313,7 +306,7 @@
         in_specs=[pl.BlockSpec(memory_space=pltpu.SMEM)] + [hbm] * len(operands),
         out_specs=(vmem, vmem),
         scratch_shapes=[pltpu.VMEM(x.shape, x.dtype) for x in operands] + [
-            pltpu.SemaphoreType.DMA((len(operands) - 2 + 2 * (blocks // LANES),)),
+            pltpu.SemaphoreType.DMA((len(operands),)),
             pltpu.VMEM((tokens // (2 * LANES), rank, 2 * LANES), BF16),
             pltpu.VMEM((tokens // (2 * LANES), heads * HEAD_SIZE, 2 * LANES), BF16),
             pltpu.VMEM((heads * HEAD_SIZE, rank), BF16),
@@ -459,7 +452,7 @@
         keep_ref[m] = one(2 * m + par)
         return _
 
-    lax.fori_loop(0, n // 2, step, 0, unroll=2)
+    lax.fori_loop(0, n // 2, step, 0, unroll=min(8, n // 2))
 
 
 def holder(par, w, v, share, combos):

time: 50.7 us -> 48.7 us (0.961)
  Pallas kernels: 23.3 us -> 21.3 us
    pallas_call x1, Pallas kernels: 10.5 us -> 8.87 us  [owner(): pl.pallas_call(functools.partial(owner_kernel, share, pool, n), out_shape...]
where the time goes in v5:
time: 48.7 us; the launch traced here: 48.5 us
  Pallas kernels  21.3 us (44%)
  blocking collectives  12.1 us (25%)
  starting transfers between devices  7.46 us (15%)
  waiting for transfers between devices  6.1 us (13%)
  between operations  0.73 us (1%)
  local copies, waits for them, and re-layouts  0.63 us (1%)
    all_to_all x1, blocking collectives, per_device(): lax.all_to_all(both, 'store', split_axis=0, concat_axis=0, tiled=True, ax...  12.1 us
    pallas_call x1, Pallas kernels, owner(): pl.pallas_call(functools.partial(owner_kernel, share, pool, n), out_shape...  8.87 us
    all_to_all x1, starting transfers between devices, per_device(): w = lax.all_to_all(w, 'store', split_axis=0, concat_axis=0, tiled=True)  7.39 us
    pallas_call x1, Pallas kernels, holder(): pl.pallas_call(functools.partial(holder_kernel, share, combos), out_shape...  6.52 us
    pallas_call x1, Pallas kernels, tile_rows(): pl.pallas_call(tile_kernel, out_shape=jax.ShapeDtypeStruct(shape, v.dtype...  5.96 us
    all_to_all x1, waiting for transfers between devices, per_device(): w = lax.all_to_all(w, 'store', split_axis=0, concat_axis=0, tiled=True)  4.58 us
    ppermute x1, waiting for transfers between devices, per_device(): other = lax.ppermute(send, 'store', [(i, i ^ 1) for i in range(n)])  1.52 us
  transfers between devices with their start and end apart: 2, of which 2 were waited for; matrix products, arithmetic and copies ran while one was open for 0% of the time, Pallas kernels for 12%

profile of v5, /device:TPU:0, one launch (start us, length us, event | category | flops | bytes accessed | tf_op | source)
XLA Modules:
  0.0 48.5 jit_solution(13178811442356192088)
XLA Ops:
  0.7 8.9 %owner.1 = (bf16[16,72,128]{2,1,0:T(8,128)(2,1)}, f32[128,128]{1,0:T(8,128)}) custom-call(s32[1]{0:T(128)S(6)} %copy.12.len_ref, bf16[2,8192]{1,0:T(2,128)(2,1)} %bitcast.12, bf16[2,1024]{1,0:T(2,128)(2,1)} %bitcast.15, bf16[2,1024]{1,0:T(2,128)(2,1)} %bitcast.16, bf16[160,4096]{1,0:T(8,128)(2,1)} %bitcast.10, bf16[160,1024]{1,0:T(8,128)(2,1)} %bitcast.11, ...), custom_call_target="tpu_custom_call" | custom-call | tf_op jit(solution)/shard_map/owner/pallas_call | solution.py:303
  9.5 7.4 %all-to-all-start = ((bf16[16,72,128]{2,1,0:T(8,128)(2,1)}), bf16[16,72,128]{2,1,0:T(8,128)(2,1)S(1)}, u32[]{:S(2)}, u32[]{:S(2)}) async-start(bf16[16,72,128]{2,1,0:T(8,128)(2,1)} %get-tuple-element.13), calls=%async_computation | async-start | bytes 589824 | tf_op jit(solution)/shard_map/all_to_all | solution.py:500
  16.9 6.0 %tile_rows.1.v_hbm = bf16[4096,8,128]{2,1,0:T(8,128)(2,1)} custom-call(bf16[4096,1024]{1,0:T(8,128)(2,1)} %v_hbm), custom_call_target="tpu_custom_call" | custom-call | flops 2147483648 | bytes 16777216 | tf_op jit(solution)/shard_map/tile_rows/pallas_call | solution.py:382
  22.9 0.0 copy-start
  22.9 4.6 %all-to-all-done.w_ref = bf16[16,72,128]{2,1,0:T(8,128)(2,1)S(1)} async-done(((bf16[16,72,128]{2,1,0:T(8,128)(2,1)}), bf16[16,72,128]{2,1,0:T(8,128)(2,1)S(1)}, u32[]{:S(2)}, u32[]{:S(2)}) %all-to-all-start) | async-done | bytes 294944 | tf_op jit(solution)/shard_map/all_to_all | solution.py:500
  27.5 6.5 %holder.1 = (f32[8,128,128]{2,1,0:T(8,128)S(1)}, bf16[8,128,128]{2,1,0:T(8,128)(2,1)S(1)}) custom-call(s32[1]{0:T(128)} %bitcast.8.par_ref, bf16[16,72,128]{2,1,0:T(8,128)(2,1)S(1)} %all-to-all-done.w_ref, bf16[4096,8,128]{2,1,0:T(8,128)(2,1)} %tile_rows.1.v_hbm), custom_call_target="tpu_custom_call" | custom-call | tf_op jit(solution)/shard_map/holder/pallas_call | solution.py:463
  34.0 0.1 collective-permute-start
  34.1 1.5 %collective-permute-done = bf16[8,128,128]{2,1,0:T(8,128)(2,1)S(1)} collective-permute-done((bf16[8,128,128]{2,1,0:T(8,128)(2,1)S(1)}, bf16[8,128,128]{2,1,0:T(8,128)(2,1)S(1)}, u32[]{:S(2)}, u32[]{:S(2)}) %collective-permute-start) | collective-permute-done | bytes 262176 | tf_op jit(solution)/shard_map/ppermute | solution.py:503
  35.6 0.1 add_convert_fusion
  35.7 12.1 %all_to_all.10 = bf16[8,128,128]{2,1,0:T(8,128)(2,1)S(1)} all-to-all(bf16[8,128,128]{2,1,0:T(8,128)(2,1)S(1)} %add_convert_fusion), channel_id=1, replica_groups={{0,2,4,6,8,10,12,14},{1,3,5,7,9,11,13,15},{16,18,20,22,24,26,28,30},{17..., dimensions={0} | all-to-all | bytes 524288 | tf_op jit(solution)/shard_map/all_to_all | solution.py:506
  47.8 0.0 copy-done
  47.9 0.6 %reshape.11 = bf16[2,1,8192]{2,0,1:T(2,128)(2,1)} reshape(bf16[128,128]{1,0:T(8,128)(2,1)S(1)} %add_convert_fusion.1) | data formatting | bytes 65536 | tf_op jit(solution)/shard_map/reshape | solution.py:508
  (2 shorter events, 0.0 us)
Async XLA Ops:
  9.5 18.0 %all-to-all-start = ((bf16[16,72,128]{2,1,0:T(8,128)(2,1)}), bf16[16,72,128]{2,1,0:T(8,128)(2,1)S(1)}, u32[]{:S(2)}, u32[]{:S(2)}) async-start(bf16[16,72,128]{2,1,0:T(8,128)(2,1)} %get-tuple-element.13), calls=%async_computation | async-start | bytes 589824 | tf_op jit(solution)/shard_map/all_to_all | solution.py:500
  22.9 24.9 %copy-start = (f32[128,128]{1,0:T(8,128)S(1)}, f32[128,128]{1,0:T(8,128)}, u32[]{:S(2)}) copy-start(f32[128,128]{1,0:T(8,128)} %get-tuple-element.11) | copy-start | bytes 196612
  34.0 1.6 %collective-permute-start = (bf16[8,128,128]{2,1,0:T(8,128)(2,1)S(1)}, bf16[8,128,128]{2,1,0:T(8,128)(2,1)S(1)}, u32[]{:S(2)}, u32[]{:S(2)}) collective-permute-start(bf16[8,128,128]{2,1,0:T(8,128)(2,1)S(1)} %get-tuple-element.16), channel_id=1, source_target_pairs={{0,1},{1,0},{2,3},{3,2},{4,5},{5,4},{6,7},{7,6},{8,9},{9,8},{10,11... | collective-permute-start | bytes 786440 | tf_op jit(solution)/shard_map/ppermute | solution.py:503

commit v6 on v5

--- a/solution.py
+++ b/solution.py
@@ -46,9 +46,9 @@
 
 def owner_kernel(
     share, pool, keepers, len_ref, q_hbm, nk_hbm, iv_hbm, kl_hbm, rk_hbm, sm_hbm, ch_hbm, tab_hbm, turn_hbm,
-    w_ref, fresh_ref,
+    w_hbm, fresh_ref,
     q_ref, nk_ref, iv_ref, kl_ref, rk_ref, sm_ref, ch_ref, tab_ref, turn_ref, sems,
-    lp, kk, rt, qp, qr, nr, vr, sc, fs_scr, fm_scr, fw_scr, pm, got_scr, lhs_scr, osc,
+    lp, kk, rt, qp, qr, nr, vr, sc, fs_scr, fm_scr, fw_scr, pm, got_scr, lhs_scr, osc, w_ref, w_sems,
 ):
     rank, tokens = kl_ref.shape
     heads, blocks = sm_ref.shape
@@ -278,12 +278,20 @@
     fresh_ref[...] = mm(fw_scr[...].astype(BF16), vr[...].astype(BF16))
 
     turned = [osc[t].T for t in range(planes)]
-    if share % 8 == 0:
-        for k in range(keepers):
+    size = w_ref.shape[0] // w_sems.shape[0]
+    sends = []
+    for k in range(w_ref.shape[0]):
+        if share % 8 == 0:
             w_ref[k] = jnp.concatenate([t[k * share:(k + 1) * share, :] for t in turned], axis=0).astype(BF16)
-    else:
-        for t in range(planes):
-            w_ref[t] = turned[t].astype(BF16)
+        else:
+            w_ref[k] = turned[k].astype(BF16)
+        if (k + 1) % size == 0:
+            at = pl.ds(k + 1 - size, size)
+            send = pltpu.make_async_copy(w_ref.at[at], w_hbm.at[at], w_sems.at[k // size])
+            send.start()
+            sends.append(send)
+    for send in sends:
+        send.wait()
 
 
 def owner(length, q, nk, iv, kl, rk, sm, ch, share, n, pool):
@@ -304,7 +312,7 @@
         functools.partial(owner_kernel, share, pool, n),
         out_shape=(jax.ShapeDtypeStruct(w_shape, BF16), jax.ShapeDtypeStruct((rows, HEAD_SIZE), F32)),
         in_specs=[pl.BlockSpec(memory_space=pltpu.SMEM)] + [hbm] * len(operands),
-        out_specs=(vmem, vmem),
+        out_specs=(hbm, vmem),
         scratch_shapes=[pltpu.VMEM(x.shape, x.dtype) for x in operands] + [
             pltpu.SemaphoreType.DMA((len(operands),)),
             pltpu.VMEM((tokens // (2 * LANES), rank, 2 * LANES), BF16),
@@ -322,6 +330,8 @@
             pltpu.VMEM((heads, 16 + 3 * rows // heads * BLOCK_TOKENS, combos // heads * n_sel), F32),
             pltpu.VMEM((heads, (planes + 1) * rows // combos, combos // heads * n_sel), BF16),
             pltpu.VMEM((planes, rows, slots), F32),
+            pltpu.VMEM(w_shape, BF16),
+            pltpu.SemaphoreType.DMA((2 if direct else 1,)),
         ],
         compiler_params=pltpu.CompilerParams(vmem_limit_bytes=60 * 1024 * 1024),
         name="owner",

time: 48.7 us -> 49.3 us (1.012)
  Pallas kernels: 21.3 us -> 21.9 us
    pallas_call x1, Pallas kernels: 8.87 us -> 9.49 us  [owner(): pl.pallas_call(functools.partial(owner_kernel, share, pool, n), out_shape...]
where the time goes in v6:
time: 49.3 us; the launch traced here: 49.1 us
  Pallas kernels  21.9 us (44%)
  blocking collectives  12.1 us (25%)
  starting transfers between devices  7.45 us (15%)
  waiting for transfers between devices  6.15 us (12%)
  between operations  0.73 us (1%)
  local copies, waits for them, and re-layouts  0.63 us (1%)
    all_to_all x1, blocking collectives, per_device(): lax.all_to_all(both, 'store', split_axis=0, concat_axis=0, tiled=True, ax...  12.1 us
    pallas_call x1, Pallas kernels, owner(): pl.pallas_call(functools.partial(owner_kernel, share, pool, n), out_shape...  9.49 us
    all_to_all x1, starting transfers between devices, per_device(): w = lax.all_to_all(w, 'store', split_axis=0, concat_axis=0, tiled=True)  7.38 us
    pallas_call x1, Pallas kernels, holder(): pl.pallas_call(functools.partial(holder_kernel, share, combos), out_shape...  6.51 us
    pallas_call x1, Pallas kernels, tile_rows(): pl.pallas_call(tile_kernel, out_shape=jax.ShapeDtypeStruct(shape, v.dtype...  5.91 us
    all_to_all x1, waiting for transfers between devices, per_device(): w = lax.all_to_all(w, 'store', split_axis=0, concat_axis=0, tiled=True)  4.63 us
    ppermute x1, waiting for transfers between devices, per_device(): other = lax.ppermute(send, 'store', [(i, i ^ 1) for i in range(n)])  1.52 us
  transfers between devices with their start and end apart: 2, of which 2 were waited for; matrix products, arithmetic and copies ran while one was open for 0% of the time, Pallas kernels for 12%

profile of v6, /device:TPU:0, one launch (start us, length us, event | category | flops | bytes accessed | tf_op | source)
XLA Modules:
  0.0 49.1 jit_solution(11846501211432015370)
XLA Ops:
  0.7 9.5 %owner.1 = (bf16[16,72,128]{2,1,0:T(8,128)(2,1)}, f32[128,128]{1,0:T(8,128)}) custom-call(s32[1]{0:T(128)S(6)} %copy.12.len_ref, bf16[2,8192]{1,0:T(2,128)(2,1)} %bitcast.12, bf16[2,1024]{1,0:T(2,128)(2,1)} %bitcast.15, bf16[2,1024]{1,0:T(2,128)(2,1)} %bitcast.16, bf16[160,4096]{1,0:T(8,128)(2,1)} %bitcast.10, bf16[160,1024]{1,0:T(8,128)(2,1)} %bitcast.11, ...), custom_call_target="tpu_custom_call" | custom-call | tf_op jit(solution)/shard_map/owner/pallas_call | solution.py:311
  10.2 7.4 %all-to-all-start = ((bf16[16,72,128]{2,1,0:T(8,128)(2,1)}), bf16[16,72,128]{2,1,0:T(8,128)(2,1)S(1)}, u32[]{:S(2)}, u32[]{:S(2)}) async-start(bf16[16,72,128]{2,1,0:T(8,128)(2,1)} %get-tuple-element.13), calls=%async_computation | async-start | bytes 589824 | tf_op jit(solution)/shard_map/all_to_all | solution.py:510
  17.5 5.9 %tile_rows.1.v_hbm = bf16[4096,8,128]{2,1,0:T(8,128)(2,1)} custom-call(bf16[4096,1024]{1,0:T(8,128)(2,1)} %v_hbm), custom_call_target="tpu_custom_call" | custom-call | flops 2147483648 | bytes 16777216 | tf_op jit(solution)/shard_map/tile_rows/pallas_call | solution.py:392
  23.5 0.0 copy-start
  23.5 4.6 %all-to-all-done.w_ref = bf16[16,72,128]{2,1,0:T(8,128)(2,1)S(1)} async-done(((bf16[16,72,128]{2,1,0:T(8,128)(2,1)}), bf16[16,72,128]{2,1,0:T(8,128)(2,1)S(1)}, u32[]{:S(2)}, u32[]{:S(2)}) %all-to-all-start) | async-done | bytes 294944 | tf_op jit(solution)/shard_map/all_to_all | solution.py:510
  28.1 6.5 %holder.1 = (f32[8,128,128]{2,1,0:T(8,128)S(1)}, bf16[8,128,128]{2,1,0:T(8,128)(2,1)S(1)}) custom-call(s32[1]{0:T(128)} %bitcast.8.par_ref, bf16[16,72,128]{2,1,0:T(8,128)(2,1)S(1)} %all-to-all-done.w_ref, bf16[4096,8,128]{2,1,0:T(8,128)(2,1)} %tile_rows.1.v_hbm), custom_call_target="tpu_custom_call" | custom-call | tf_op jit(solution)/shard_map/holder/pallas_call | solution.py:473
  34.6 0.1 collective-permute-start
  34.7 1.5 %collective-permute-done = bf16[8,128,128]{2,1,0:T(8,128)(2,1)S(1)} collective-permute-done((bf16[8,128,128]{2,1,0:T(8,128)(2,1)S(1)}, bf16[8,128,128]{2,1,0:T(8,128)(2,1)S(1)}, u32[]{:S(2)}, u32[]{:S(2)}) %collective-permute-start) | collective-permute-done | bytes 262176 | tf_op jit(solution)/shard_map/ppermute | solution.py:513
  36.2 0.1 add_convert_fusion
  36.3 12.1 %all_to_all.10 = bf16[8,128,128]{2,1,0:T(8,128)(2,1)S(1)} all-to-all(bf16[8,128,128]{2,1,0:T(8,128)(2,1)S(1)} %add_convert_fusion), channel_id=1, replica_groups={{0,2,4,6,8,10,12,14},{1,3,5,7,9,11,13,15},{16,18,20,22,24,26,28,30},{17..., dimensions={0} | all-to-all | bytes 524288 | tf_op jit(solution)/shard_map/all_to_all | solution.py:516
  48.4 0.0 copy-done
  48.5 0.6 %reshape.11 = bf16[2,1,8192]{2,0,1:T(2,128)(2,1)} reshape(bf16[128,128]{1,0:T(8,128)(2,1)S(1)} %add_convert_fusion.1) | data formatting | bytes 65536 | tf_op jit(solution)/shard_map/reshape | solution.py:518
  (2 shorter events, 0.1 us)
Async XLA Ops:
  10.2 18.0 %all-to-all-start = ((bf16[16,72,128]{2,1,0:T(8,128)(2,1)}), bf16[16,72,128]{2,1,0:T(8,128)(2,1)S(1)}, u32[]{:S(2)}, u32[]{:S(2)}) async-start(bf16[16,72,128]{2,1,0:T(8,128)(2,1)} %get-tuple-element.13), calls=%async_computation | async-start | bytes 589824 | tf_op jit(solution)/shard_map/all_to_all | solution.py:510
  23.5 25.0 %copy-start = (f32[128,128]{1,0:T(8,128)S(1)}, f32[128,128]{1,0:T(8,128)}, u32[]{:S(2)}) copy-start(f32[128,128]{1,0:T(8,128)} %get-tuple-element.11) | copy-start | bytes 196612
  34.6 1.6 %collective-permute-start = (bf16[8,128,128]{2,1,0:T(8,128)(2,1)S(1)}, bf16[8,128,128]{2,1,0:T(8,128)(2,1)S(1)}, u32[]{:S(2)}, u32[]{:S(2)}) collective-permute-start(bf16[8,128,128]{2,1,0:T(8,128)(2,1)S(1)} %get-tuple-element.16), channel_id=1, source_target_pairs={{0,1},{1,0},{2,3},{3,2},{4,5},{5,4},{6,7},{7,6},{8,9},{9,8},{10,11... | collective-permute-start | bytes 786440 | tf_op jit(solution)/shard_map/ppermute | solution.py:513
